TPU v7x, 512 devices: a whole 4x8x8 slice. The times are simulated.
512 devices in a mesh: loop: 16 (over y, x_hi), dp: 32 (over z, x_lo, core).
Axes of the slice: x: 4 (x_hi: 2, x_lo: 2; x = x_hi * 2 + x_lo), y: 8, z: 8, core: 2. Of those that a mesh axis runs over, the one named last changes fastest.
Arguments:
- images: bfloat16 [32, 32, 16, 16, 768], P('dp', 'loop'), may hold values from -6 to 6
- kernel: float32 [7, 7, 768], replicated, may hold values from -0.875 to 0.875
- ln_gain: float32 [768], replicated, may hold values from 0.5 to 1.5
- w_up: bfloat16 [768, 1536], P('dp'), may hold values from -0.21875 to 0.21875
- b_up: float32 [1536], replicated, may hold values from -3 to 3
- w_down: bfloat16 [1536, 768], P('dp'), may hold values from -0.15625 to 0.15625
- layer_scale: float32 [768], replicated, may hold values from 0.3 to 1
- w_head: bfloat16 [768, 1152], P('dp'), may hold values from -0.21875 to 0.21875
- text_rows: bfloat16 [32, 32, 1152], P('dp', 'loop'), may hold values from -6 to 6
- pair_ids: int32 [32, 32], P('dp', 'loop'), may hold values from 0 to 31, each once within a row
- log_temp: float32 [1], replicated, may hold values from 1.5 to 2.5
- loss_bias: float32 [1], replicated, may hold values from -6 to -2
Outputs:
- kernel_grad: float32 [7, 7, 768], replicated
- up_grad: float32 [768, 1536], P('dp')
- text_grad: float32 [32, 32, 1152], P('dp', 'loop')
Inputs may be any that keep to these rules, and one draw needn't show every extreme that they name: Each row of pair_ids holds every index of its group once.
All inputs are finite; a program needn't handle non-finite values.
Results may differ from a plain program's by a relative error of at most 0.04.
Values may be sent and summed in bfloat16 or wider, within the bound.
A program may use at most 64 MiB of HBM per device.

v0:
```python
import jax
import jax.numpy as jnp
from jax import lax
from jax.sharding import PartitionSpec as P

epsilon = 1e-06


def passed_along(value, axis, steps):
    count = lax.axis_size(axis)
    pairs = [(source, (source + steps) % count) for source in range(count)]
    return lax.ppermute(value, axis, pairs)


def image_tower(kernel, w_up, images, ln_gain, b_up, w_down, layer_scale, w_head):
    image_count = images.shape[0]
    grid_side = images.shape[1]
    channels = images.shape[3]
    padded = jnp.pad(images, ((0, 0), (3, 3), (3, 3), (0, 0)))
    conv_out = jnp.zeros(images.shape, jnp.float32)
    for row_off in range(7):
        for col_off in range(7):
            window = padded[:, row_off : row_off + grid_side, col_off : col_off + grid_side, :]
            conv_out = conv_out + window.astype(jnp.float32) * kernel[row_off, col_off]
    chan_mean = jnp.mean(conv_out, axis=-1, keepdims=True)
    centered = conv_out - chan_mean
    chan_var = jnp.mean(centered * centered, axis=-1, keepdims=True)
    normed = (centered * lax.rsqrt(chan_var + epsilon) * ln_gain).astype(jnp.bfloat16)
    flat_rows = normed.reshape(-1, channels)
    hidden = jnp.dot(flat_rows, w_up, preferred_element_type=jnp.float32) + b_up
    active = jax.nn.gelu(hidden, approximate=True).astype(jnp.bfloat16)
    mlp_out = jnp.dot(active, w_down, preferred_element_type=jnp.float32)
    block_out = images.reshape(-1, channels).astype(jnp.float32) + layer_scale * mlp_out
    pooled = jnp.mean(
        block_out.reshape(image_count, grid_side * grid_side, channels), axis=1
    ).astype(jnp.bfloat16)
    embedding = jnp.dot(pooled, w_head, preferred_element_type=jnp.float32)
    return embedding * lax.rsqrt(jnp.sum(embedding * embedding, axis=-1, keepdims=True) + epsilon)


def pair_grad(image_emb, text_emb, pair_row, text_index, logit_scale, logit_bias, group_size):
    logits = (
        logit_scale * jnp.dot(image_emb, text_emb.T, precision=lax.Precision.HIGHEST) + logit_bias
    )
    sign_of = jnp.where(pair_row[:, None] == text_index[None, :], 1.0, -1.0)
    return -sign_of * jax.nn.sigmoid(-sign_of * logits) / group_size


def body(
    images,
    kernel,
    ln_gain,
    w_up,
    b_up,
    w_down,
    layer_scale,
    w_head,
    text_rows,
    pair_ids,
    log_temp,
    loss_bias,
):
    loop_size = lax.axis_size("loop")
    loop_index = lax.axis_index("loop")
    up_full, down_full, head_full = (
        lax.all_gather(w_up, "dp", axis=0, tiled=True),
        lax.all_gather(w_down, "dp", axis=0, tiled=True),
        lax.all_gather(w_head, "dp", axis=0, tiled=True),
    )
    pictures = images[0]
    pair_row = pair_ids[0]
    img_dev = pictures.shape[0]
    group_size = img_dev * loop_size
    logit_scale = jnp.exp(log_temp[0])
    logit_bias = loss_bias[0]

    def run_tower(kernel_arg, up_arg):
        return image_tower(
            kernel_arg, up_arg, pictures, ln_gain, b_up, down_full, layer_scale, head_full
        )

    image_emb, pullback = jax.vjp(run_tower, kernel, up_full)
    raw_rows = text_rows[0].astype(jnp.float32)
    text_norm = jnp.sqrt(jnp.sum(raw_rows * raw_rows, axis=-1, keepdims=True) + epsilon)
    text_hat = raw_rows / text_norm
    rounded = lax.optimization_barrier(text_hat.astype(jnp.bfloat16))
    local_index = jnp.arange(img_dev, dtype=jnp.int32)

    def cycle_step(step_index, state):
        text_block, partials, image_cot = state
        source = (loop_index - step_index) % loop_size
        text_index = source * img_dev + local_index
        pair_weight = pair_grad(
            image_emb, text_block, pair_row, text_index, logit_scale, logit_bias, group_size
        )
        image_cot = image_cot + logit_scale * jnp.dot(
            pair_weight, text_block, precision=lax.Precision.HIGHEST
        )
        partials = partials + logit_scale * jnp.dot(
            pair_weight.T, image_emb, precision=lax.Precision.HIGHEST
        )
        text_block, partials = passed_along((text_block, partials), "loop", 1)
        return (text_block, partials, image_cot)

    start = (
        rounded.astype(jnp.float32),
        jnp.zeros(raw_rows.shape, jnp.float32),
        jnp.zeros(image_emb.shape, jnp.float32),
    )
    _, text_cot, image_cot = lax.fori_loop(0, loop_size, cycle_step, start)
    text_grad = (
        text_cot - text_hat * jnp.sum(text_hat * text_cot, axis=-1, keepdims=True)
    ) / text_norm
    kernel_part, up_part = pullback(image_cot)
    kernel_grad = lax.psum(kernel_part, ("loop", "dp"))
    up_rows = lax.psum_scatter(
        up_part.astype(jnp.float32).astype(jnp.bfloat16), "dp", scatter_dimension=0, tiled=True
    )
    up_grad = lax.psum(up_rows, "loop").astype(jnp.float32)
    return (kernel_grad, up_grad, text_grad[None])


def solution(mesh):
    placed = (
        P("dp", "loop", None, None, None),
        P(),
        P(),
        P("dp", None),
        P(),
        P("dp", None),
        P(),
        P("dp", None),
        P("dp", "loop", None),
        P("dp", "loop"),
        P(),
        P(),
    )
    return jax.shard_map(
        body,
        mesh=mesh,
        in_specs=placed,
        out_specs=(P(), P("dp", None), P("dp", "loop", None)),
        check_vma=False,
    )
```

profile of v0, /device:TPU:1, one launch (start us, length us, event | category | flops | bytes accessed | tf_op | source)
XLA Modules:
  0.0 996.5 jit_solution(3485320233537033907)
XLA Ops:
  15.5 30.5 %fusion.140 = (f32[2,16,16]{2,1,0:T(8,128)S(1)}, f32[2,16,16,768]{3,2,1,0:T(8,128)S(1)}) fusion(f32[768]{0:T(1024)S(1)} %get-tuple-element.377, f32[768]{0:T(1024)S(1)} %get-tuple-element.378, f32[768]{0:T(1024)S(1)} %get-tuple-element.331, f32[768]{0:T(1024)S(1)} %get-tuple-element.332, f32[768]{0:T(1024)S(1)} %get-tuple-element.333, ...), kind=kLoop, calls=%fused_computation.374 | loop fusion | flops 57802240 | bytes 2511872 | tf_op jit(solution)/shard_map/jvp()/reduce_sum | solution.py:25
  46.7 37.7 %all-gather.4.cloned.1.call-done = bf16[768,1536]{1,0:T(8,128)(2,1)} async-done(((bf16[24,1536]{1,0:T(8,128)(2,1)}), bf16[768,1536]{1,0:T(8,128)(2,1)}) %all-gather.4.cloned.1.call-update) | async-done | bytes 2359312 | tf_op jit(solution)/shard_map/all_gather | solution.py:66
  84.4 4.8 convolution_add_fusion
  89.2 65.1 %all-gather.6.cloned.1.call-done = bf16[1536,768]{1,0:T(8,128)(2,1)} async-done(((bf16[48,768]{1,0:T(8,128)(2,1)}), bf16[1536,768]{1,0:T(8,128)(2,1)}) %all-gather.6.cloned.1.call-update) | async-done | bytes 2359312 | tf_op jit(solution)/shard_map/all_gather | solution.py:67
  154.3 4.6 bitcast_reduce_fusion
  158.9 64.5 %all-gather.8.cloned.1.call-done = bf16[768,1152]{1,0:T(8,128)(2,1)} async-done(((bf16[24,1152]{1,0:T(8,128)(2,1)}), bf16[768,1152]{1,0:T(8,128)(2,1)}) %all-gather.8.cloned.1.call-update) | async-done | bytes 1769488 | tf_op jit(solution)/shard_map/all_gather | solution.py:68
  225.4 184.7 %while.20 = (s32[]{:T(128)}, f32[2,1152]{1,0:T(2,128)S(1)}, f32[2,1152]{1,0:T(2,128)S(1)}, f32[2,1152]{1,0:T(2,128)S(1)}, f32[]{:T(128)}, /*index=5*/s32[1,2]{1,...) while((s32[]{:T(128)}, f32[2,1152]{1,0:T(2,128)S(1)}, ...), condition=%wide.region_6.7_spmd.clone, body=%wide.region_5.6_spmd.clone.sunk | while | flops 177470 | bytes 166336 | solution.py:110
  225.5 4.3 collective-permute-start
  230.9 3.4 collective-permute-start.1
  234.5 4.4 collective-permute-done.1
  242.0 4.6 collective-permute-start.1
  246.8 3.2 collective-permute-done.1
  253.7 3.4 collective-permute-start.1
  257.3 4.4 collective-permute-done.1
  264.8 4.6 collective-permute-start.1
  269.5 3.2 collective-permute-done.1
  276.4 3.4 collective-permute-start.1
  280.0 4.4 collective-permute-done.1
  287.5 4.6 collective-permute-start.1
  292.3 3.2 collective-permute-done.1
  299.1 5.2 collective-permute-start.1
  307.1 3.1 collective-permute-start
  311.4 6.0 collective-permute-start.1
  319.4 3.9 collective-permute-start
  324.4 3.9 collective-permute-start.1
  328.5 4.0 collective-permute-done.1
  335.6 3.8 collective-permute-start.1
  339.6 4.1 collective-permute-done.1
  346.7 3.8 collective-permute-start.1
  350.7 4.1 collective-permute-done.1
  357.8 3.8 collective-permute-start.1
  361.8 4.1 collective-permute-done.1
  368.9 3.8 collective-permute-start.1
  372.8 4.1 collective-permute-done.1
  380.0 3.8 collective-permute-start.1
  384.0 4.0 collective-permute-done.1
  391.1 3.8 collective-permute-start.1
  395.0 4.1 collective-permute-done.1
  402.2 4.1 collective-permute-start.1
  406.5 3.7 collective-permute-done.1
  412.6 4.6 fusion.14
  421.3 3.6 fusion.143
  426.0 5.0 fusion.117
  431.1 3.7 fusion.23
  434.9 3.9 fusion.118
  440.1 119.1 %reduce-scatter.2.cloned.1.call-done = bf16[24,1536]{1,0:T(8,128)(2,1)} async-done(((bf16[768,1536]{1,0:T(8,128)(2,1)}), bf16[24,1536]{1,0:T(8,128)(2,1)}) %reduce-scatter.2.cloned.1.call-update) | async-done | bytes 73744 | tf_op jit(solution)/shard_map/reduce_scatter | solution.py:116
  560.5 148.9 %all-reduce.55.cloned.1.call-done = bf16[24,1536]{1,0:T(8,128)(2,1)} async-done(((bf16[24,1536]{1,0:T(8,128)(2,1)}), bf16[24,1536]{1,0:T(8,128)(2,1)}) %all-reduce.55.cloned.1.call-update) | async-done | bytes 73744 | tf_op jit(solution)/shard_map/psum | solution.py:119
  711.0 277.1 %all-reduce.53.cloned.1.call-done = f32[7,7,768]{2,1,0:T(8,128)} async-done(((f32[7,7,768]{2,1,0:T(8,128)}), f32[7,7,768]{2,1,0:T(8,128)}) %all-reduce.53.cloned.1.call-update) | async-done | bytes 150544 | tf_op jit(solution)/shard_map/psum | solution.py:115
  (216 shorter events, 74.9 us)
Async XLA Ops:
  7.2 77.2 %all-gather.4.cloned.1.call-start = ((), (), s32[]{:S(2)}) async-start(), calls=%async_computation.1 | async-start | bytes 2433024 | tf_op jit(solution)/shard_map/all_gather | solution.py:66
  7.9 146.4 %all-gather.6.cloned.1.call-start = ((), (), s32[]{:S(2)}) async-start(), calls=%async_computation.2 | async-start | bytes 2433024 | tf_op jit(solution)/shard_map/all_gather | solution.py:67
  8.6 214.8 %all-gather.8.cloned.1.call-start = ((), (), s32[]{:S(2)}) async-start(), calls=%async_computation.3 | async-start | bytes 1824768 | tf_op jit(solution)/shard_map/all_gather | solution.py:68
  9.4 549.9 %reduce-scatter.2.cloned.1.call-start = ((), (), s32[]{:S(2)}) async-start(), calls=%async_computation.5 | async-start | bytes 2433024 | tf_op jit(solution)/shard_map/reduce_scatter | solution.py:116
  15.5 30.9 %copy-start.1 = (f32[768]{0:T(1024)S(1)}, f32[768]{0:T(1024)}, u32[]{:S(2)}) copy-start(f32[768]{0:T(1024)} %param.16) | copy-start | bytes 9220
  46.4 38.0 %copy-start.4 = (f32[1536]{0:T(1024)S(1)}, f32[1536]{0:T(1024)}, u32[]{:S(2)}) copy-start(f32[1536]{0:T(1024)} %param.18) | copy-start | bytes 18436
  84.4 69.9 %copy-start = (bf16[1,2,16,16,768]{4,3,2,1,0:T(8,128)(2,1)S(1)}, bf16[1,2,16,16,768]{4,3,2,1,0:T(8,128)(2,1)}, u32[]{:S(2)}) copy-start(bf16[1,2,16,16,768]{4,3,2,1,0:T(8,128)(2,1)} %param.14) | copy-start | bytes 2359300
  84.4 69.9 %copy-start.2 = (f32[768]{0:T(1024)S(1)}, f32[768]{0:T(1024)}, u32[]{:S(2)}) copy-start(f32[768]{0:T(1024)} %param.20) | copy-start | bytes 9220
  158.9 66.5 %copy-start.5 = (s32[1,2]{1,0:T(1,128)S(1)}, s32[1,2]{1,0:T(1,128)}, u32[]{:S(2)}) copy-start(s32[1,2]{1,0:T(1,128)} %param.23) | copy-start | bytes 28
  225.5 13.5 %collective-permute-start = (f32[2,1152]{1,0:T(2,128)S(1)}, f32[2,1152]{1,0:T(2,128)S(1)}, u32[]{:S(2)}, u32[]{:S(2)}) collective-permute-start(f32[2,1152]{1,0:T(2,128)S(1)} %copy.20), channel_id=1, source_target_pairs={{0,32},{32,64},{64,96},{96,128},{128,160},{160,192},{192,224},{224... | collective-permute-start | bytes 27656 | tf_op jit(solution)/shard_map/while/body/eval_jaxpr/ppermute | solution.py:12
  230.9 8.0 collective-permute-start.1
  239.0 11.1 %collective-permute-start = (f32[2,1152]{1,0:T(2,128)S(1)}, f32[2,1152]{1,0:T(2,128)S(1)}, u32[]{:S(2)}, u32[]{:S(2)}) collective-permute-start(f32[2,1152]{1,0:T(2,128)S(1)} %copy.20), channel_id=1, source_target_pairs={{0,32},{32,64},{64,96},{96,128},{128,160},{160,192},{192,224},{224... | collective-permute-start | bytes 27656 | tf_op jit(solution)/shard_map/while/body/eval_jaxpr/ppermute | solution.py:12
  242.0 8.0 collective-permute-start.1
  250.1 11.6 %collective-permute-start = (f32[2,1152]{1,0:T(2,128)S(1)}, f32[2,1152]{1,0:T(2,128)S(1)}, u32[]{:S(2)}, u32[]{:S(2)}) collective-permute-start(f32[2,1152]{1,0:T(2,128)S(1)} %copy.20), channel_id=1, source_target_pairs={{0,32},{32,64},{64,96},{96,128},{128,160},{160,192},{192,224},{224... | collective-permute-start | bytes 27656 | tf_op jit(solution)/shard_map/while/body/eval_jaxpr/ppermute | solution.py:12
  253.7 8.0 collective-permute-start.1
  261.7 11.1 %collective-permute-start = (f32[2,1152]{1,0:T(2,128)S(1)}, f32[2,1152]{1,0:T(2,128)S(1)}, u32[]{:S(2)}, u32[]{:S(2)}) collective-permute-start(f32[2,1152]{1,0:T(2,128)S(1)} %copy.20), channel_id=1, source_target_pairs={{0,32},{32,64},{64,96},{96,128},{128,160},{160,192},{192,224},{224... | collective-permute-start | bytes 27656 | tf_op jit(solution)/shard_map/while/body/eval_jaxpr/ppermute | solution.py:12
  264.8 8.0 collective-permute-start.1
  272.8 11.6 %collective-permute-start = (f32[2,1152]{1,0:T(2,128)S(1)}, f32[2,1152]{1,0:T(2,128)S(1)}, u32[]{:S(2)}, u32[]{:S(2)}) collective-permute-start(f32[2,1152]{1,0:T(2,128)S(1)} %copy.20), channel_id=1, source_target_pairs={{0,32},{32,64},{64,96},{96,128},{128,160},{160,192},{192,224},{224... | collective-permute-start | bytes 27656 | tf_op jit(solution)/shard_map/while/body/eval_jaxpr/ppermute | solution.py:12
  276.4 8.0 collective-permute-start.1
  284.4 11.1 %collective-permute-start = (f32[2,1152]{1,0:T(2,128)S(1)}, f32[2,1152]{1,0:T(2,128)S(1)}, u32[]{:S(2)}, u32[]{:S(2)}) collective-permute-start(f32[2,1152]{1,0:T(2,128)S(1)} %copy.20), channel_id=1, source_target_pairs={{0,32},{32,64},{64,96},{96,128},{128,160},{160,192},{192,224},{224... | collective-permute-start | bytes 27656 | tf_op jit(solution)/shard_map/while/body/eval_jaxpr/ppermute | solution.py:12
  287.5 8.0 collective-permute-start.1
  295.5 11.6 %collective-permute-start = (f32[2,1152]{1,0:T(2,128)S(1)}, f32[2,1152]{1,0:T(2,128)S(1)}, u32[]{:S(2)}, u32[]{:S(2)}) collective-permute-start(f32[2,1152]{1,0:T(2,128)S(1)} %copy.20), channel_id=1, source_target_pairs={{0,32},{32,64},{64,96},{96,128},{128,160},{160,192},{192,224},{224... | collective-permute-start | bytes 27656 | tf_op jit(solution)/shard_map/while/body/eval_jaxpr/ppermute | solution.py:12
  299.1 8.0 collective-permute-start.1
  307.1 12.3 %collective-permute-start = (f32[2,1152]{1,0:T(2,128)S(1)}, f32[2,1152]{1,0:T(2,128)S(1)}, u32[]{:S(2)}, u32[]{:S(2)}) collective-permute-start(f32[2,1152]{1,0:T(2,128)S(1)} %copy.20), channel_id=1, source_target_pairs={{0,32},{32,64},{64,96},{96,128},{128,160},{160,192},{192,224},{224... | collective-permute-start | bytes 27656 | tf_op jit(solution)/shard_map/while/body/eval_jaxpr/ppermute | solution.py:12
  311.4 8.0 collective-permute-start.1
  319.4 13.1 %collective-permute-start = (f32[2,1152]{1,0:T(2,128)S(1)}, f32[2,1152]{1,0:T(2,128)S(1)}, u32[]{:S(2)}, u32[]{:S(2)}) collective-permute-start(f32[2,1152]{1,0:T(2,128)S(1)} %copy.20), channel_id=1, source_target_pairs={{0,32},{32,64},{64,96},{96,128},{128,160},{160,192},{192,224},{224... | collective-permute-start | bytes 27656 | tf_op jit(solution)/shard_map/while/body/eval_jaxpr/ppermute | solution.py:12
  324.4 8.0 collective-permute-start.1
  332.5 11.2 %collective-permute-start = (f32[2,1152]{1,0:T(2,128)S(1)}, f32[2,1152]{1,0:T(2,128)S(1)}, u32[]{:S(2)}, u32[]{:S(2)}) collective-permute-start(f32[2,1152]{1,0:T(2,128)S(1)} %copy.20), channel_id=1, source_target_pairs={{0,32},{32,64},{64,96},{96,128},{128,160},{160,192},{192,224},{224... | collective-permute-start | bytes 27656 | tf_op jit(solution)/shard_map/while/body/eval_jaxpr/ppermute | solution.py:12
  335.6 8.0 collective-permute-start.1
  343.7 11.1 %collective-permute-start = (f32[2,1152]{1,0:T(2,128)S(1)}, f32[2,1152]{1,0:T(2,128)S(1)}, u32[]{:S(2)}, u32[]{:S(2)}) collective-permute-start(f32[2,1152]{1,0:T(2,128)S(1)} %copy.20), channel_id=1, source_target_pairs={{0,32},{32,64},{64,96},{96,128},{128,160},{160,192},{192,224},{224... | collective-permute-start | bytes 27656 | tf_op jit(solution)/shard_map/while/body/eval_jaxpr/ppermute | solution.py:12
  346.7 8.0 collective-permute-start.1
  354.7 11.1 %collective-permute-start = (f32[2,1152]{1,0:T(2,128)S(1)}, f32[2,1152]{1,0:T(2,128)S(1)}, u32[]{:S(2)}, u32[]{:S(2)}) collective-permute-start(f32[2,1152]{1,0:T(2,128)S(1)} %copy.20), channel_id=1, source_target_pairs={{0,32},{32,64},{64,96},{96,128},{128,160},{160,192},{192,224},{224... | collective-permute-start | bytes 27656 | tf_op jit(solution)/shard_map/while/body/eval_jaxpr/ppermute | solution.py:12
  357.8 8.0 collective-permute-start.1
  365.8 11.1 %collective-permute-start = (f32[2,1152]{1,0:T(2,128)S(1)}, f32[2,1152]{1,0:T(2,128)S(1)}, u32[]{:S(2)}, u32[]{:S(2)}) collective-permute-start(f32[2,1152]{1,0:T(2,128)S(1)} %copy.20), channel_id=1, source_target_pairs={{0,32},{32,64},{64,96},{96,128},{128,160},{160,192},{192,224},{224... | collective-permute-start | bytes 27656 | tf_op jit(solution)/shard_map/while/body/eval_jaxpr/ppermute | solution.py:12
  368.9 8.0 collective-permute-start.1
  376.9 11.1 %collective-permute-start = (f32[2,1152]{1,0:T(2,128)S(1)}, f32[2,1152]{1,0:T(2,128)S(1)}, u32[]{:S(2)}, u32[]{:S(2)}) collective-permute-start(f32[2,1152]{1,0:T(2,128)S(1)} %copy.20), channel_id=1, source_target_pairs={{0,32},{32,64},{64,96},{96,128},{128,160},{160,192},{192,224},{224... | collective-permute-start | bytes 27656 | tf_op jit(solution)/shard_map/while/body/eval_jaxpr/ppermute | solution.py:12
  380.0 8.0 collective-permute-start.1
  388.0 11.1 %collective-permute-start = (f32[2,1152]{1,0:T(2,128)S(1)}, f32[2,1152]{1,0:T(2,128)S(1)}, u32[]{:S(2)}, u32[]{:S(2)}) collective-permute-start(f32[2,1152]{1,0:T(2,128)S(1)} %copy.20), channel_id=1, source_target_pairs={{0,32},{32,64},{64,96},{96,128},{128,160},{160,192},{192,224},{224... | collective-permute-start | bytes 27656 | tf_op jit(solution)/shard_map/while/body/eval_jaxpr/ppermute | solution.py:12
  391.1 8.0 collective-permute-start.1
  399.1 11.1 %collective-permute-start = (f32[2,1152]{1,0:T(2,128)S(1)}, f32[2,1152]{1,0:T(2,128)S(1)}, u32[]{:S(2)}, u32[]{:S(2)}) collective-permute-start(f32[2,1152]{1,0:T(2,128)S(1)} %copy.20), channel_id=1, source_target_pairs={{0,32},{32,64},{64,96},{96,128},{128,160},{160,192},{192,224},{224... | collective-permute-start | bytes 27656 | tf_op jit(solution)/shard_map/while/body/eval_jaxpr/ppermute | solution.py:12
  402.2 8.0 collective-permute-start.1
  410.2 2.4 copy-start.3
  417.2 1.2 copy-start.6
  421.2 288.2 %all-reduce.55.cloned.1.call-start = ((), (), s32[]{:S(2)}) async-start(), calls=%async_computation.6 | async-start | bytes 147456 | tf_op jit(solution)/shard_map/psum | solution.py:119
  559.3 428.8 %all-reduce.53.cloned.1.call-start = ((), (), s32[]{:S(2)}) async-start(), calls=%async_computation.4 | async-start | bytes 344064 | tf_op jit(solution)/shard_map/psum | solution.py:115
Sparse Core Ops, SparseCore 0:
  10.1 74.2 all-gather.3
  86.5 67.7 all-gather.5
  156.5 66.9 all-gather.7
  421.4 137.8 reduce-scatter.1
  562.0 147.3 all-reduce.54
  715.6 272.4 all-reduce.52
where the time goes:
time: 998 us; the launch traced here: 997 us
  waiting for transfers between devices  774 us (78%)
  starting transfers between devices  104 us (10%)
  other arithmetic  50 us (5%)
  matrix products  44.9 us (4%)
  between operations  15.4 us (2%)
    psum x1, waiting for transfers between devices, body(): kernel_grad = lax.psum(kernel_part, ('loop', 'dp'))  277 us
    psum x1, waiting for transfers between devices, body(): up_grad = lax.psum(up_rows, 'loop').astype(jnp.float32)  149 us
    reduce_scatter x1, waiting for transfers between devices, body(): lax.psum_scatter(up_part.astype(jnp.float32).astype(jnp.bfloat16), 'dp',...  119 us
    ppermute x32, starting transfers between devices, passed_along(): return lax.ppermute(value, axis, pairs)  104 us
    all_gather x1, waiting for transfers between devices, body(): lax.all_gather(w_down, 'dp', axis=0, tiled=True)  65.1 us
    all_gather x1, waiting for transfers between devices, body(): lax.all_gather(w_head, 'dp', axis=0, tiled=True)  64.5 us
    ppermute x32, waiting for transfers between devices, passed_along(): return lax.ppermute(value, axis, pairs)  59.5 us
    all_gather x1, waiting for transfers between devices, body(): lax.all_gather(w_up, 'dp', axis=0, tiled=True)  37.7 us
  transfers between devices with their start and end apart: 38, of which 22 were waited for; matrix products, arithmetic and copies ran while one was open for 9% of the time, Pallas kernels for 0%

commit v1 on v0

v1 whole, which is shorter than its diff:
```python
import functools

import jax
import jax.numpy as jnp
from jax import lax
from jax.experimental import pallas as pl
from jax.experimental.pallas import tpu as pltpu
from jax.sharding import PartitionSpec as P

MESH = pl.DeviceIdType.MESH
EPS = 1e-06
BF = jnp.bfloat16
F32 = jnp.float32
HI = lax.Precision.HIGHEST

N_LOOP = 16
N_DP = 32
N_Z = 8
C = 768
FFW = 1536
E = 1152
EH = 640
GROUP = 32
N_PIECE = 12
N_SLAB = 21


def nt(a, b, precision=None):
    return lax.dot_general(
        a, b, (((1,), (1,)), ((), ())), preferred_element_type=F32, precision=precision
    )


def tn(a, b):
    return lax.dot_general(a, b, (((0,), (0,)), ((), ())), preferred_element_type=F32)


def kernel_body(
    images,
    kern,
    gain,
    w_up,
    b_up,
    w_down,
    scale,
    w_head,
    text,
    pair,
    log_temp,
    loss_bias,
    kernel_out,
    up_out,
    text_out,
    up_pre,
    head_pre,
    up_buf,
    down_buf,
    head_buf,
    text_buf,
    text_all,
    taps,
    shifted,
    conv_pad,
    img_sum,
    normed,
    xhat,
    rstd,
    hid,
    gprime,
    dact,
    dhid,
    g_buf,
    rs1,
    s1,
    rs2,
    s2,
    rs3,
    p3,
    rs4,
    r4,
    fin,
    msg_buf,
    msg_all,
    kg,
    kr1,
    k1,
    kr2,
    kfin,
    w_send,
    w_recv,
    pre_send,
    pre_recv,
    text_send,
    text_recv,
    msg_send,
    msg_recv,
    r1_send,
    r1_recv,
    r2_send,
    r2_recv,
    r3_send,
    r3_recv,
    r4_send,
    r4_recv,
    r5_send,
    r5_recv,
    p1_send,
    p1_recv,
    p2_send,
    p2_recv,
    p3_send,
    p3_recv,
):
    me_loop = lax.axis_index("loop")
    me_dp = lax.axis_index("dp")
    core = lax.rem(me_dp, 2)
    xlo = lax.rem(me_dp // 2, 2)
    zed = me_dp // 4
    chip = me_dp // 2
    xhi = lax.rem(me_loop, 2)
    sib_dp = me_dp + 1 - 2 * core
    xnb_dp = me_dp + 2 - 4 * xlo
    loop_b = me_loop + 1 - 2 * xhi
    sgn = 1 - 2 * core

    def z_dp(offset):
        return lax.rem(zed + offset + N_Z, N_Z) * 4 + xlo * 2 + core

    def remote(src, dst, send, recv, loop, dp):
        return pltpu.make_async_remote_copy(
            src_ref=src,
            dst_ref=dst,
            send_sem=send,
            recv_sem=recv,
            device_id=(loop, dp),
            device_id_type=MESH,
        )

    barrier = pltpu.get_barrier_semaphore()

    @pl.loop(1, N_DP)
    def _(o):
        pl.semaphore_signal(
            barrier, inc=1, device_id=(me_loop, lax.rem(me_dp + o, N_DP)), device_id_type=MESH
        )

    @pl.loop(1, N_LOOP)
    def _(o):
        other = lax.rem(me_loop + o, N_LOOP)
        pl.semaphore_signal(barrier, inc=1, device_id=(other, me_dp), device_id_type=MESH)
        pl.semaphore_signal(barrier, inc=1, device_id=(other, sib_dp), device_id_type=MESH)

    pl.semaphore_signal(barrier, inc=1, device_id=(loop_b, xnb_dp), device_id_type=MESH)

    zero8 = jnp.zeros((8, C), F32)
    for half in range(2):
        rows = w_up[:, half * C : (half + 1) * C].astype(F32)
        up_pre[0, half] = jnp.concatenate([rows, zero8], axis=0).astype(BF)
    zero8 = jnp.zeros((8, EH), F32)
    rows = w_head[:, :EH].astype(F32)
    head_pre[0, 0] = jnp.concatenate([rows, zero8], axis=0).astype(BF)
    rows = w_head[:, EH:].astype(F32)
    rows = jnp.concatenate([rows, jnp.zeros((24, 2 * EH - E), F32)], axis=1)
    head_pre[0, 1] = jnp.concatenate([rows, zero8], axis=0).astype(BF)
    down_buf[chip, core] = w_down[...]
    text_buf[me_loop] = text[...].astype(F32)

    pl.semaphore_wait(barrier, N_DP - 1 + 2 * (N_LOOP - 1) + 1)

    slab_of = (
        lambda c, where: up_buf.at[c, where],
        lambda c, where: down_buf.at[where, c],
        lambda c, where: head_buf.at[c, where],
    )
    pending = []

    def send(copy):
        copy.start()
        pending.append(copy)

    def to_sibling(w, owner_core, where, sem):
        slab = slab_of[w](owner_core, where)
        send(remote(slab, slab, w_send.at[w, sem], w_recv.at[w, sem], me_loop, sib_dp))

    def to_x(w, where_z, sem):
        slab = slab_of[w](core, where_z * 2 + xlo)
        side = lax.rem(where_z, 2)
        target = me_loop + side * (loop_b - me_loop)
        send(remote(slab, slab, w_send.at[w, sem], w_recv.at[w, sem], target, xnb_dp))

    def to_z(w, where_z, direction, sem):
        slab = slab_of[w](core, where_z * 2 + xlo)
        send(
            remote(
                slab, slab, w_send.at[w, sem], w_recv.at[w, sem], me_loop, z_dp(direction * sgn)
            )
        )

    def await_slab(w, owner_core, where, sem):
        slab = slab_of[w](owner_core, where)
        remote(slab, slab, w_send.at[w, sem], w_recv.at[w, sem], me_loop, sib_dp).wait_recv()

    def kind_z(kind):
        offset = -kind if kind <= 4 else kind - 4
        return lax.rem(zed + offset * sgn + N_Z, N_Z)

    def begin(w):
        to_z(w, zed, 1, 0)
        to_z(w, zed, -1, 4)
        to_x(w, zed, 7)
        to_sibling(w, core, chip, 15)

    def z_arrival(w, kind):
        sem = kind - 1
        where_z = kind_z(kind)
        await_slab(w, core, where_z * 2 + xlo, sem)
        if kind in (1, 2, 3):
            to_z(w, where_z, 1, sem + 1)
        if kind in (5, 6):
            to_z(w, where_z, -1, sem + 1)
        to_x(w, where_z, 7 + kind)
        to_sibling(w, core, where_z * 2 + xlo, 15 + kind)

    def x_arrival(w, kind):
        where = kind_z(kind) * 2 + 1 - xlo
        await_slab(w, core, where, 7 + kind)
        to_sibling(w, core, where, 23 + kind)

    def turn(w, step):
        if step <= 4:
            z_arrival(w, step)
        if step <= 3:
            z_arrival(w, 4 + step)
        if step == 1:
            x_arrival(w, 0)
        if 2 <= step <= 5:
            x_arrival(w, step - 1)
        if 2 <= step <= 4:
            x_arrival(w, 3 + step)

    def finish(w):
        for kind in range(8):
            await_slab(w, 1 - core, kind_z_other(kind) * 2 + xlo, 15 + kind)
            await_slab(w, 1 - core, kind_z_other(kind) * 2 + 1 - xlo, 23 + kind)

    def kind_z_other(kind):
        offset = -kind if kind <= 4 else kind - 4
        return lax.rem(zed - offset * sgn + N_Z, N_Z)

    pre = []
    for index, ref in ((0, up_pre), (1, head_pre)):
        copy = remote(
            ref.at[0, 1 - core],
            ref.at[1, 0],
            pre_send.at[index],
            pre_recv.at[index],
            me_loop,
            sib_dp,
        )
        copy.start()
        pre.append(copy)
        if index == 0:
            begin(1)

    def text_copy(o):
        return remote(
            text_buf.at[me_loop],
            text_buf.at[me_loop],
            text_send.at[o],
            text_recv.at[o],
            lax.rem(me_loop + o, N_LOOP),
            me_dp,
        )

    def merge(index, ref, width):
        pre[index].wait_recv()
        mine = ref[0, core].astype(F32)[:24]
        theirs = ref[1, 0].astype(F32)[:24]
        first = core == 0
        joined = jnp.concatenate(
            [jnp.where(first, mine, theirs), jnp.where(first, theirs, mine)], axis=0
        )
        return joined.astype(BF)

    up_buf[core, chip] = merge(0, up_pre, C)
    begin(0)
    head_buf[core, chip] = merge(1, head_pre, EH)
    begin(2)

    @pl.loop(1, N_LOOP)
    def _(o):
        text_copy(o).start()

    width_at = lax.broadcasted_iota(jnp.int32, (16, 128), 0)

    def chunk_lanes(cb):
        return pl.ds(pl.multiple_of(cb * 128, 128), 128)

    def conv_chunk(chunk, carry):
        image, cb = chunk // 6, lax.rem(chunk, 6)
        lanes = chunk_lanes(cb)
        for a in range(7):
            for b in range(7):
                taps[a * 7 + b] = jnp.broadcast_to(kern[a, pl.ds(b, 1), lanes], (8, 128))

        def row(r, state):
            accs, total = state
            x = images[image, r, :, lanes].astype(F32)
            views = []
            for b in range(7):
                if b == 3:
                    view = x
                else:
                    view = pltpu.roll(x, (3 - b) % 16, 0)
                    inside = width_at >= 3 - b if b < 3 else width_at < 19 - b
                    view = jnp.where(inside, view, 0.0)
                shifted[chunk, b, r] = view
                views.append(view.reshape(2, 8, 128))
            fresh = []
            for j in range(7):
                acc = accs[j]
                for b in range(7):
                    acc = acc + views[b] * taps[(6 - j) * 7 + b]
                fresh.append(acc)
            conv_pad[image, r, :, lanes] = fresh[0].reshape(16, 128)
            return (tuple(fresh[1:]) + (jnp.zeros((2, 8, 128), F32),), total + views[3])

        zero = jnp.zeros((2, 8, 128), F32)
        accs, total = lax.fori_loop(0, 16, row, ((zero,) * 7, zero))
        for j in range(3):
            conv_pad[image, 16 + j, :, lanes] = accs[j].reshape(16, 128)
        img_sum[image, :, lanes] = total[0] + total[1]
        return carry

    plan = (
        ((0, 1), (1, 1)),
        ((2, 1), (0, 2)),
        ((1, 2), (2, 2), (0, 3)),
        ((1, 3), (0, 4)),
        ((2, 3), (0, 5)),
        ((1, 4), (2, 4)),
    )
    for group in range(6):
        lax.fori_loop(2 * group, 2 * group + 2, conv_chunk, 0)
        for w, step in plan[group]:
            turn(w, step)

    gain_row = gain[...]

    def norm_rows(index, carry):
        image, r = index // 16, lax.rem(index, 16)
        rows = pl.ds(pl.multiple_of(index * 16, 16), 16)
        value = conv_pad[image, r + 3]
        centered = value - jnp.mean(value, axis=-1, keepdims=True)
        inv = lax.rsqrt(jnp.mean(centered * centered, axis=-1, keepdims=True) + EPS)
        hat = centered * inv
        xhat[rows, :] = hat
        rstd[rows, :] = jnp.broadcast_to(inv, (16, 128))
        normed[rows, :] = (hat * gain_row).astype(BF)
        return carry

    lax.fori_loop(0, 32, norm_rows, 0)
    finish(0)

    c0 = 0.7978845608028654
    row_at = lax.broadcasted_iota(jnp.int32, (16, C), 0)
    means = []
    for half in range(2):
        hid[...] = jnp.dot(
            normed[...], up_buf[half].reshape(C, C), preferred_element_type=F32
        )
        if half == 0:
            turn(1, 5)
        else:
            turn(2, 5)
        bias = b_up[:, half * C : (half + 1) * C]
        image_sums = []
        for image in range(2):

            def gelu_rows(index, total):
                rows = pl.ds(pl.multiple_of(image * 256 + index * 16, 16), 16)
                h = hid[rows, :] + bias
                square = h * h
                t = jnp.tanh(c0 * h * (1.0 + 0.044715 * square))
                plus = 0.5 + 0.5 * t
                active = (h * plus).astype(BF).astype(F32)
                gprime[half, rows, :] = plus + (0.5 * c0) * h * (1.0 - t * t) * (
                    1.0 + (3 * 0.044715) * square
                )
                return total + active[:8] + active[8:]

            total = lax.fori_loop(0, 16, gelu_rows, jnp.zeros((8, C), F32))
            image_sums.append(jnp.sum(total, axis=0, keepdims=True) * (1.0 / 256))
        means.append(
            jnp.where(row_at == 0, image_sums[0], jnp.where(row_at == 1, image_sums[1], 0.0))
        )

    finish(1)
    mlp = jnp.zeros((16, C), F32)
    for half in range(2):
        high = means[half].astype(BF)
        low = (means[half] - high.astype(F32)).astype(BF)
        rows = down_buf[8 * half : 8 * half + 8].reshape(C, C)
        mlp = mlp + jnp.dot(high, rows, preferred_element_type=F32)
        mlp = mlp + jnp.dot(low, rows, preferred_element_type=F32)
    img_mean = [jnp.sum(img_sum[image], axis=0, keepdims=True) * (1.0 / 256) for image in range(2)]
    img_mean = jnp.where(row_at == 0, img_mean[0], jnp.where(row_at == 1, img_mean[1], 0.0))
    pooled = (img_mean + scale[...] * mlp).astype(BF)
    finish(2)
    raw = [
        jnp.dot(pooled, head_buf[half].reshape(C, EH), preferred_element_type=F32)
        for half in range(2)
    ]
    norm = lax.rsqrt(
        jnp.sum(raw[0] * raw[0], axis=-1, keepdims=True)
        + jnp.sum(raw[1] * raw[1], axis=-1, keepdims=True)
        + EPS
    )
    emb = jnp.concatenate([raw[0] * norm, raw[1][:, : E - EH] * norm], axis=1)

    @pl.loop(1, N_LOOP)
    def _(o):
        text_copy(o).wait_recv()

    for l in range(N_LOOP):
        text_all[2 * l : 2 * l + 2, :] = text_buf[l]
    raw_rows = text_all[...]
    text_norm = jnp.sqrt(jnp.sum(raw_rows * raw_rows, axis=-1, keepdims=True) + EPS)
    text_emb = (raw_rows / text_norm).astype(BF).astype(F32)
    logit_scale = jnp.exp(jnp.full((1, 1), log_temp[0], F32))
    logits = logit_scale * nt(emb, text_emb, HI) + loss_bias[0]
    pair_row_at = lax.broadcasted_iota(jnp.int32, (16, GROUP), 0)
    pair_col_at = lax.broadcasted_iota(jnp.int32, (16, GROUP), 1)
    own = jnp.where(pair_row_at == 0, pair[0, 0], pair[0, 1])
    signs = jnp.where(own == pair_col_at, 1.0, -1.0)
    weight = -signs * jax.nn.sigmoid(-signs * logits) / GROUP
    weight = jnp.where(pair_row_at < 2, weight, 0.0)
    image_cot = logit_scale * jnp.dot(weight, text_emb, precision=HI, preferred_element_type=F32)

    msg_buf[me_loop, :, :E] = emb[:2]
    msg_buf[me_loop, :, E:] = jnp.concatenate(
        [weight[:2], jnp.zeros((2, 128 - GROUP), F32)], axis=1
    )

    def msg_copy(o):
        return remote(
            msg_buf.at[me_loop],
            msg_buf.at[me_loop],
            msg_send.at[o],
            msg_recv.at[o],
            lax.rem(me_loop + o, N_LOOP),
            me_dp,
        )

    @pl.loop(1, N_LOOP)
    def _(o):
        msg_copy(o).start()

    d_raw = norm * (image_cot - emb * jnp.sum(image_cot * emb, axis=-1, keepdims=True))
    d_raw = d_raw.astype(BF)
    d_pooled = nt(d_raw[:, :EH], head_buf[0].reshape(C, EH)) + nt(
        d_raw[:, EH:], head_buf[1, :, :, : E - EH].reshape(C, E - EH)
    )
    d_pooled = d_pooled.astype(BF).astype(F32)
    d_mlp = (scale[...] * (d_pooled * (1.0 / 256))).astype(BF)
    for half in range(2):
        value = nt(d_mlp, down_buf[8 * half : 8 * half + 8].reshape(C, C))
        dact[half] = value.astype(BF).astype(F32)

    def hidden_cot(half):
        for image in range(2):
            factor = dact[half, image : image + 1, :]

            def rows_cot(index, carry):
                rows = pl.ds(pl.multiple_of(image * 256 + index * 16, 16), 16)
                dhid[half, rows, :] = (gprime[half, rows, :] * factor).astype(BF)
                return carry

            lax.fori_loop(0, 16, rows_cot, 0)

    def up_grad_half(half):
        hidden_cot(half)
        g_buf[half] = tn(normed[...], dhid[half]).astype(BF).reshape(16, 48, C)

    up_grad_half(1 - core)
    r1 = []
    for part in range(2):
        chips = pl.ds(8 * part, 8)
        copy = remote(
            g_buf.at[1 - core, chips],
            rs1.at[chips],
            r1_send.at[part],
            r1_recv.at[part],
            me_loop,
            sib_dp,
        )
        send(copy)
        r1.append(copy)
    up_grad_half(core)
    for copy in r1:
        copy.wait_recv()

    def core_sum(where):
        s1[where] = (g_buf[core, where].astype(F32) + rs1[where].astype(F32)).astype(BF)

    def x_copy(z):
        where = z * 2 + 1 - xlo
        target = me_loop + lax.rem(z, 2) * (loop_b - me_loop)
        return remote(s1.at[where], rs2.at[z], r2_send.at[z], r2_recv.at[z], target, xnb_dp)

    @pl.loop(1, N_Z + 1)
    def _(o):
        z = lax.rem(zed + o, N_Z)
        core_sum(z * 2 + 1 - xlo)
        x_copy(z).start()

    @pl.loop(0, N_Z)
    def _(z):
        core_sum(z * 2 + xlo)

    hid[...] = nt(dhid[0], up_buf[0].reshape(C, C)) + nt(dhid[1], up_buf[1].reshape(C, C))

    dpad = conv_pad
    for image in range(2):
        for j in (0, 1, 2, 19, 20, 21, 22):
            dpad[image, j] = jnp.zeros((16, C), F32)

    def norm_cot(index, carry):
        rows = pl.ds(pl.multiple_of(index * 16, 16), 16)
        d_hat = hid[rows, :].astype(BF).astype(F32) * gain_row
        hat = xhat[rows, :]
        first = jnp.mean(d_hat, axis=-1, keepdims=True)
        second = jnp.mean(d_hat * hat, axis=-1, keepdims=True)
        dpad[index // 16, lax.rem(index, 16) + 3] = rstd[rows, :1] * (
            d_hat - first - hat * second
        )
        return carry

    lax.fori_loop(0, 32, norm_cot, 0)

    def z_copy(o):
        z = lax.rem(zed + o, N_Z)
        return remote(
            s2.at[z],
            rs3.at[o - 1],
            r3_send.at[o - 1],
            r3_recv.at[o - 1],
            me_loop,
            z * 4 + xlo * 2 + core,
        )

    def x_sum(z):
        x_copy(z).wait_recv()
        s2[z] = (s1[z * 2 + xlo].astype(F32) + rs2[z].astype(F32)).astype(BF)

    @pl.loop(1, N_Z)
    def _(o):
        x_sum(lax.rem(zed + o, N_Z))
        z_copy(o).start()

    x_sum(zed)

    kg[...] = jnp.zeros(kg.shape, F32)

    def slab_copy(slab):
        return remote(
            kg.at[slab], kr1.at[me_dp], p1_send.at[slab], p1_recv.at[me_dp], me_loop, slab
        )

    tap_at = lax.broadcasted_iota(jnp.int32, (8, 128), 0)

    def kernel_chunk(cb, offset):
        lanes = chunk_lanes(cb)

        def column(b, carry):
            accs = [jnp.zeros((2, 8, 128), F32) for _ in range(7)]
            for image in range(2):

                def row(r, state):
                    view = shifted[image * 6 + cb, b, r].reshape(2, 8, 128)
                    window = state[0]
                    accs = [state[1][a] + view * window[6 - a] for a in range(7)]
                    ahead = dpad[image, r + 7, :, lanes].reshape(2, 8, 128)
                    return (window[1:] + (ahead,), tuple(accs))

                window = tuple(
                    dpad[image, j, :, lanes].reshape(2, 8, 128) for j in range(7)
                )
                _, accs = lax.fori_loop(0, 16, row, (window, tuple(accs)))
            slab0 = (cb // 2) * 7
            for a in range(7):
                value = jnp.sum(accs[a][0] + accs[a][1], axis=0, keepdims=True)
                columns = slice(offset, offset + 128)
                kg[slab0 + a, :, columns] = kg[slab0 + a, :, columns] + jnp.where(
                    tap_at == b, value, 0.0
                )
            return carry

        lax.fori_loop(0, 7, column, 0)

    for group in range(3):
        kernel_chunk(2 * group, 0)
        kernel_chunk(2 * group + 1, 128)
        for a in range(7):
            slab = group * 7 + a

            @pl.when(me_dp != slab)
            def _():
                slab_copy(slab).start()

    total = s2[zed].astype(F32)
    for o in range(1, N_Z):
        z_copy(o).wait_recv()
        total = total + rs3[o - 1].astype(F32)
    for q in range(N_PIECE):
        rb, lh = q // 2, q % 2
        p3[q] = total[rb * 8 : rb * 8 + 8, lh * 384 : lh * 384 + 384]

    def piece_copy(q):
        return remote(p3.at[q], rs4.at[me_loop], r4_send.at[q], r4_recv.at[me_loop], q, me_dp)

    for q in range(N_PIECE):

        @pl.when(me_loop != q)
        def _():
            piece_copy(q).start()

    def p1_wait(o):
        other = lax.rem(me_dp + o, N_DP)
        remote(
            kr1.at[other], kr1.at[other], p1_send.at[0], p1_recv.at[other], me_loop, sib_dp
        ).wait_recv()
        return other

    def share_copy(o):
        return remote(
            kr2.at[me_loop],
            kr2.at[me_loop],
            p2_send.at[o],
            p2_recv.at[o],
            lax.rem(me_loop + o, N_LOOP),
            me_dp,
        )

    @pl.when(me_dp < N_SLAB)
    def _():
        k1[...] = kg[me_dp]

        @pl.loop(1, N_DP)
        def _(o):
            other = p1_wait(o)
            k1[...] = k1[...] + kr1[other]

        kr2[me_loop] = k1[...]

        @pl.loop(1, N_LOOP)
        def _(o):
            share_copy(o).start()

    target_core = me_loop // 6
    target_dp = chip * 2 + target_core
    own_piece = lax.rem(me_loop, 6)

    def result_copy(o):
        return remote(
            r4,
            fin.at[core, own_piece],
            r5_send.at[o],
            r5_recv.at[core, own_piece],
            lax.rem(me_loop + o, N_LOOP),
            target_dp,
        )

    @pl.when(me_loop < N_PIECE)
    def _():
        r4[...] = p3[me_loop]

        @pl.loop(1, N_LOOP)
        def _(o):
            other = lax.rem(me_loop + o, N_LOOP)
            remote(
                rs4.at[other], rs4.at[other], r4_send.at[0], r4_recv.at[other], me_loop, sib_dp
            ).wait_recv()
            r4[...] = r4[...] + rs4[other]

        @pl.loop(1, N_LOOP)
        def _(o):
            result_copy(o).start()

        @pl.when(target_core != core)
        def _():
            remote(
                r4,
                fin.at[core, own_piece],
                r5_send.at[0],
                r5_recv.at[core, own_piece],
                me_loop,
                sib_dp,
            ).start()

        @pl.when(target_core == core)
        def _():
            fin[core, own_piece] = r4[...]

    def spread_copy(o):
        return remote(
            k1,
            kfin.at[me_dp],
            p3_send.at[o],
            p3_recv.at[me_dp],
            me_loop,
            lax.rem(me_dp + o, N_DP),
        )

    @pl.when(me_dp < N_SLAB)
    def _():
        @pl.loop(1, N_LOOP)
        def _(o):
            share_copy(o).wait_recv()

        summed = kr2[0]
        for l in range(1, N_LOOP):
            summed = summed + kr2[l]
        k1[...] = summed

        @pl.loop(1, N_DP)
        def _(o):
            spread_copy(o).start()

        kfin[me_dp] = summed

    @pl.loop(1, N_LOOP)
    def _(o):
        msg_copy(o).wait_recv()

    for l in range(N_LOOP):
        msg_all[2 * l : 2 * l + 2, :] = msg_buf[l]
    all_emb = msg_all[:, :E]
    all_weight = msg_all[:, E:]
    pick_row = lax.broadcasted_iota(jnp.int32, (8, 128), 0)
    pick_col = lax.broadcasted_iota(jnp.int32, (8, 128), 1)
    pick = jnp.where((pick_col == 2 * me_loop + pick_row) & (pick_row < 2), 1.0, 0.0)
    mine = nt(pick, all_weight, HI)
    text_cot = logit_scale * jnp.dot(mine, all_emb, precision=HI, preferred_element_type=F32)
    text_cot = text_cot[:2]
    own_rows = text[...].astype(F32)
    own_norm = jnp.sqrt(jnp.sum(own_rows * own_rows, axis=-1, keepdims=True) + EPS)
    own_hat = own_rows / own_norm
    text_out[...] = (
        text_cot - own_hat * jnp.sum(own_hat * text_cot, axis=-1, keepdims=True)
    ) / own_norm

    for cs in range(2):
        for j in range(6):

            @pl.when((core * 6 + j != me_loop) | (core != cs))
            def _():
                remote(
                    r4, fin.at[cs, j], r5_send.at[0], r5_recv.at[cs, j], me_loop, sib_dp
                ).wait_recv()

            rb, lh = j // 2, j % 2
            up_out[rb * 8 : rb * 8 + 8, cs * C + lh * 384 : cs * C + lh * 384 + 384] = fin[cs, j]

    for slab in range(N_SLAB):

        @pl.when(me_dp != slab)
        def _():
            remote(
                k1, kfin.at[slab], p3_send.at[0], p3_recv.at[slab], me_loop, sib_dp
            ).wait_recv()

        lp, a = slab // 7, slab % 7
        kernel_out[a, :, lp * 256 : lp * 256 + 256] = kfin[slab, :7]

    for copy in pending:
        copy.wait_send()
    for copy in pre:
        copy.wait_send()

    @pl.loop(1, N_LOOP)
    def _(o):
        text_copy(o).wait_send()
        msg_copy(o).wait_send()

    @pl.loop(0, N_Z)
    def _(z):
        x_copy(z).wait_send()

    @pl.loop(1, N_Z)
    def _(o):
        z_copy(o).wait_send()

    for slab in range(N_SLAB):

        @pl.when(me_dp != slab)
        def _():
            slab_copy(slab).wait_send()

    for q in range(N_PIECE):

        @pl.when(me_loop != q)
        def _():
            piece_copy(q).wait_send()

    @pl.when(me_loop < N_PIECE)
    def _():
        @pl.loop(1, N_LOOP)
        def _(o):
            result_copy(o).wait_send()

        @pl.when(target_core != core)
        def _():
            result_copy(0).wait_send()

    @pl.when(me_dp < N_SLAB)
    def _():
        @pl.loop(1, N_LOOP)
        def _(o):
            share_copy(o).wait_send()

        @pl.loop(1, N_DP)
        def _(o):
            spread_copy(o).wait_send()


def body(
    images,
    kernel,
    ln_gain,
    w_up,
    b_up,
    w_down,
    layer_scale,
    w_head,
    text_rows,
    pair_ids,
    log_temp,
    loss_bias,
):
    vmem = pl.BlockSpec(memory_space=pltpu.VMEM)
    smem = pl.BlockSpec(memory_space=pltpu.SMEM)
    dma = pltpu.SemaphoreType.DMA
    scratch = [
        pltpu.VMEM((2, 2, 32, C), BF),
        pltpu.VMEM((2, 2, 32, EH), BF),
        pltpu.VMEM((2, 16, 48, C), BF),
        pltpu.VMEM((16, 2, 48, C), BF),
        pltpu.VMEM((2, 16, 48, EH), BF),
        pltpu.VMEM((N_LOOP, 2, E), F32),
        pltpu.VMEM((GROUP, E), F32),
        pltpu.VMEM((49, 8, 128), F32),
        pltpu.VMEM((12, 7, 16, 16, 128), F32),
        pltpu.VMEM((2, 23, 16, C), F32),
        pltpu.VMEM((2, 8, C), F32),
        pltpu.VMEM((512, C), BF),
        pltpu.VMEM((512, C), F32),
        pltpu.VMEM((512, 128), F32),
        pltpu.VMEM((512, C), F32),
        pltpu.VMEM((2, 512, C), F32),
        pltpu.VMEM((2, 16, C), F32),
        pltpu.VMEM((2, 512, C), BF),
        pltpu.VMEM((2, 16, 48, C), BF),
        pltpu.VMEM((16, 48, C), BF),
        pltpu.VMEM((16, 48, C), BF),
        pltpu.VMEM((8, 48, C), BF),
        pltpu.VMEM((8, 48, C), BF),
        pltpu.VMEM((7, 48, C), BF),
        pltpu.VMEM((N_PIECE, 8, 384), F32),
        pltpu.VMEM((N_LOOP, 8, 384), F32),
        pltpu.VMEM((8, 384), F32),
        pltpu.VMEM((2, 6, 8, 384), F32),
        pltpu.VMEM((N_LOOP, 2, E + 128), F32),
        pltpu.VMEM((GROUP, E + 128), F32),
        pltpu.VMEM((N_SLAB, 8, 256), F32),
        pltpu.VMEM((N_DP, 8, 256), F32),
        pltpu.VMEM((8, 256), F32),
        pltpu.VMEM((N_LOOP, 8, 256), F32),
        pltpu.VMEM((N_SLAB, 8, 256), F32),
        dma((3, 31)),
        dma((3, 31)),
        dma((2,)),
        dma((2,)),
        dma((N_LOOP,)),
        dma((N_LOOP,)),
        dma((N_LOOP,)),
        dma((N_LOOP,)),
        dma((2,)),
        dma((2,)),
        dma((N_Z,)),
        dma((N_Z,)),
        dma((N_Z,)),
        dma((N_Z,)),
        dma((N_LOOP,)),
        dma((N_LOOP,)),
        dma((N_LOOP,)),
        dma((2, 6)),
        dma((N_DP,)),
        dma((N_DP,)),
        dma((N_LOOP,)),
        dma((N_LOOP,)),
        dma((N_DP,)),
        dma((N_DP,)),
    ]
    kernel_grad, up_grad, text_grad = pl.pallas_call(
        kernel_body,
        out_shape=(
            jax.ShapeDtypeStruct((7, 7, C), F32),
            jax.ShapeDtypeStruct((24, FFW), F32),
            jax.ShapeDtypeStruct((2, E), F32),
        ),
        in_specs=[vmem] * 9 + [smem] * 3,
        out_specs=(vmem, vmem, vmem),
        scratch_shapes=scratch,
        compiler_params=pltpu.CompilerParams(
            collective_id=0, has_side_effects=True, vmem_limit_bytes=56 * 1024 * 1024
        ),
        name="tower_step",
    )(
        images[0],
        kernel,
        ln_gain.reshape(1, C),
        w_up,
        b_up.reshape(1, FFW),
        w_down,
        layer_scale.reshape(1, C),
        w_head,
        text_rows[0],
        pair_ids,
        log_temp,
        loss_bias,
    )
    return (kernel_grad, up_grad, text_grad[None])


def solution(mesh):
    placed = (
        P("dp", "loop", None, None, None),
        P(),
        P(),
        P("dp", None),
        P(),
        P("dp", None),
        P(),
        P("dp", None),
        P("dp", "loop", None),
        P("dp", "loop"),
        P(),
        P(),
    )
    return jax.shard_map(
        body,
        mesh=mesh,
        in_specs=placed,
        out_specs=(P(), P("dp", None), P("dp", "loop", None)),
        check_vma=False,
    )
```

time: 998 us -> 123 us (0.12)
  waiting for transfers between devices: 774 us -> 0 us
  Pallas kernels: 0 us -> 116 us
  starting transfers between devices: 104 us -> 0 us
  other arithmetic: 50 us -> 0 us
  matrix products: 44.9 us -> 0 us
  between operations: 15.4 us -> 1.99 us
    psum x2 -> x0, waiting for transfers between devices: 426 us -> none  [the longest x1 277 us: body(): kernel_grad = lax.psum(kernel_part, ('loop', 'dp'))]
    all_gather x3 -> x0, waiting for transfers between devices: 167 us -> none  [the longest x1 65.1 us: body(): lax.all_gather(w_down, 'dp', axis=0, tiled=True)]
    reduce_scatter x1 -> x0, waiting for transfers between devices: 119 us -> none  [body(): lax.psum_scatter(up_part.astype(jnp.float32).astype(jnp.bfloat16), 'dp',...]
    pallas_call x0 -> x1, Pallas kernels: none -> 116 us  [body(): pl.pallas_call(kernel_body, out_shape=(jax.ShapeDtypeStruct((7, 7, C), F3...]
    ppermute x32 -> x0, starting transfers between devices: 104 us -> none  [passed_along(): return lax.ppermute(value, axis, pairs)]
    ppermute x32 -> x0, waiting for transfers between devices: 59.5 us -> none  [passed_along(): return lax.ppermute(value, axis, pairs)]
    reduce_sum x10 -> x0, other arithmetic: 45.5 us -> none  [the longest x1 30.5 us: image_tower(): chan_mean = jnp.mean(conv_out, axis=-1, keepdims=True)]
    dot_general x55 -> x0, matrix products: 44.9 us -> none  [the longest x16 13.6 us: pair_grad(): jnp.dot(image_emb, text_emb.T, precision=lax.Precision.HIGHEST)]
  transfers between devices with their start and end apart: 38 -> 0, of which waited for: 22 -> 0; matrix products, arithmetic and copies ran while one was open for 9% -> 0% of each run, Pallas kernels for 0% -> 0%
where the time goes in v1:
time: 123 us; the launch traced here: 122 us
  Pallas kernels  116 us (94%)
  local copies, waits for them, and re-layouts  4.78 us (4%)
  between operations  1.99 us (2%)
    pallas_call x1, Pallas kernels, body(): pl.pallas_call(kernel_body, out_shape=(jax.ShapeDtypeStruct((7, 7, C), F3...  116 us
    unnamed x13, local copies, waits for them, and re-layouts  3.02 us

profile of v1, /device:TPU:1, one launch (start us, length us, event | category | flops | bytes accessed | tf_op | source)
XLA Modules:
  0.0 122.3 jit_solution(4450411614053362647)
XLA Ops:
  0.6 0.0 copy-start.3
  1.9 0.0 copy-start.4
  2.0 0.0 copy-start.2
  2.0 0.0 copy-done.3
  2.0 0.6 reshape.15.gain
  2.6 0.1 copy-done.4
  2.6 0.6 reshape.17.scale
  3.2 0.0 copy-done.2
  3.2 0.6 reshape.16.b_up
  3.8 115.5 %tower_step.1 = (f32[7,7,768]{2,1,0:T(8,128)}, f32[24,1536]{1,0:T(8,128)}, f32[2,1152]{1,0:T(2,128)}) custom-call(bf16[2,16,16,768]{3,2,1,0:T(8,128)(2,1)} %bitcast.3, f32[7,7,768]{2,1,0:T(8,128)} %kern.1, f32[1,768]{1,0:T(1,128)} %reshape.15.gain, bf16[24,1536]{1,0:T(8,128)(2,1)} %w_up.1, f32[1,1536]{1,0:T(1,128)} %reshape.16.b_up, bf16[48,768]{1,0:T(8,128)(2,1)} %w_down.1, ...), custom_call_target="tpu_custom_call" | custom-call | tf_op jit(solution)/shard_map/tower_step/pallas_call | solution.py:905
  119.3 0.0 copy-start
  119.4 1.6 %copy.20 = f32[7,7,768]{2,1,0:T(8,128)} copy(f32[7,7,768]{2,1,0:T(8,128)} %get-tuple-element.12) | data formatting | bytes 301056
  121.0 0.0 copy-done
  121.0 0.0 copy-start.1
  121.0 0.7 copy.21
  121.7 0.0 copy-done.1
  121.7 0.6 copy.22
Async XLA Ops:
  0.6 1.3 %copy-start.3 = (f32[768]{0:T(1024)S(1)}, f32[768]{0:T(1024)}, u32[]{:S(2)}) copy-start(f32[768]{0:T(1024)} %param.14) | copy-start | bytes 9220
  1.9 0.7 copy-start.4
  2.0 1.3 %copy-start.2 = (f32[1536]{0:T(1024)S(1)}, f32[1536]{0:T(1024)}, u32[]{:S(2)}) copy-start(f32[1536]{0:T(1024)} %param.16) | copy-start | bytes 18436
  119.3 1.6 %copy-start = (f32[24,1536]{1,0:T(8,128)S(1)}, f32[24,1536]{1,0:T(8,128)}, u32[]{:S(2)}) copy-start(f32[24,1536]{1,0:T(8,128)} %get-tuple-element.13) | copy-start | bytes 442372
  121.0 0.7 copy-start.1

commit v2 on v1

v2 whole, which is shorter than its diff:
```python
import functools

import jax
import jax.numpy as jnp
from jax import lax
from jax.experimental import pallas as pl
from jax.experimental.pallas import tpu as pltpu
from jax.sharding import PartitionSpec as P

MESH = pl.DeviceIdType.MESH
EPS = 1e-06
BF = jnp.bfloat16
F32 = jnp.float32
HI = lax.Precision.HIGHEST

N_LOOP = 16
N_DP = 32
N_Z = 8
C = 768
FFW = 1536
E = 1152
EH = 640
GROUP = 32
N_PIECE = 12
N_SLAB = 21


def nt(a, b, precision=None):
    return lax.dot_general(
        a, b, (((1,), (1,)), ((), ())), preferred_element_type=F32, precision=precision
    )


def tn(a, b):
    return lax.dot_general(a, b, (((0,), (0,)), ((), ())), preferred_element_type=F32)


def kernel_body(
    images,
    kern,
    gain,
    w_up,
    b_up,
    w_down,
    scale,
    w_head,
    text,
    pair,
    log_temp,
    loss_bias,
    kernel_out,
    up_out,
    text_out,
    pre,
    up_buf,
    mix_buf,
    text_buf,
    text_all,
    taps,
    shifted,
    conv_pad,
    img_sum,
    normed,
    xhat,
    rstd,
    hid,
    gprime,
    dact,
    dhid,
    g_buf,
    rs1,
    s1,
    rs2,
    s2,
    rs3,
    p3,
    rs4,
    r4,
    fin,
    msg_buf,
    msg_all,
    kg,
    kr1,
    k1,
    kr2,
    kfin,
    w_send,
    w_recv,
    bulk_send,
    bulk_recv,
    z_send,
    x_send,
    y_send,
    y_recv,
    pre_sem,
    text_sem,
    msg_sem,
    r1_sem,
    r2_send,
    r2_recv,
    r3_sem,
    r4_sem,
    r5_sem,
    p1_sem,
    p2_sem,
    p3_sem,
):
    me_loop = lax.axis_index("loop")
    me_dp = lax.axis_index("dp")
    core = lax.rem(me_dp, 2)
    xlo = lax.rem(me_dp // 2, 2)
    zed = me_dp // 4
    chip = me_dp // 2
    xhi = lax.rem(me_loop, 2)
    sib_dp = me_dp + 1 - 2 * core
    xnb_dp = me_dp + 2 - 4 * xlo
    loop_b = me_loop + 1 - 2 * xhi
    sgn = 1 - 2 * core

    def z_dp(offset):
        return lax.rem(zed + offset + N_Z, N_Z) * 4 + xlo * 2 + core

    def remote(src, dst, send, recv, loop, dp):
        return pltpu.make_async_remote_copy(
            src_ref=src,
            dst_ref=dst,
            send_sem=send,
            recv_sem=recv,
            device_id=(loop, dp),
            device_id_type=MESH,
        )

    barrier = pltpu.get_barrier_semaphore()

    @pl.loop(1, N_DP)
    def _(o):
        pl.semaphore_signal(
            barrier, inc=1, device_id=(me_loop, lax.rem(me_dp + o, N_DP)), device_id_type=MESH
        )

    @pl.loop(1, N_LOOP)
    def _(o):
        other = lax.rem(me_loop + o, N_LOOP)
        pl.semaphore_signal(barrier, inc=1, device_id=(other, me_dp), device_id_type=MESH)
        pl.semaphore_signal(barrier, inc=1, device_id=(other, sib_dp), device_id_type=MESH)

    pl.semaphore_signal(barrier, inc=1, device_id=(loop_b, xnb_dp), device_id_type=MESH)

    zero8 = jnp.zeros((8, C), F32)
    for half in range(2):
        rows = w_up[:, half * C : (half + 1) * C].astype(F32)
        pre[0, half, 0] = jnp.concatenate([rows, zero8], axis=0).astype(BF)
        rows = w_head[:, half * EH : min((half + 1) * EH, E)].astype(F32)
        rows = jnp.concatenate([rows, jnp.zeros((24, C - rows.shape[1]), F32)], axis=1)
        pre[0, half, 1] = jnp.concatenate([rows, zero8], axis=0).astype(BF)
    text_buf[me_loop] = text[...].astype(F32)

    pl.semaphore_wait(barrier, N_DP - 1 + 2 * (N_LOOP - 1) + 1)

    def whole(ref, sem, recv_sem=None):
        return remote(ref, ref, sem, sem if recv_sem is None else recv_sem, me_loop, sib_dp)

    parity = lax.rem(me_loop // 2, 2)
    mix_of = (0, parity, 1 - parity)

    def slab_of(w, owner_core, where):
        if w == 0:
            return up_buf.at[owner_core, where]
        return mix_buf.at[mix_of[w], where, owner_core]

    def to_sibling(w, where):
        slab = slab_of(w, core, where)
        remote(slab, slab, bulk_send.at[w], bulk_recv.at[w], me_loop, sib_dp).start()

    def to_x(w, where_z, sem):
        slab = slab_of(w, core, where_z * 2 + xlo)
        side = lax.rem(where_z, 2)
        target = me_loop + side * (loop_b - me_loop)
        remote(slab, slab, x_send.at[w], w_recv.at[w, sem], target, xnb_dp).start()

    def to_z(w, where_z, direction, sem):
        slab = slab_of(w, core, where_z * 2 + xlo)
        remote(
            slab, slab, z_send.at[w], w_recv.at[w, sem], me_loop, z_dp(direction * sgn)
        ).start()

    def to_y(where, sem):
        slab = slab_of(1, core, where)
        target = lax.rem(me_loop + 2 * sgn + N_LOOP, N_LOOP)
        remote(slab, slab, y_send, y_recv.at[sem], target, me_dp).start()

    def await_slab(w, where, sem):
        slab = slab_of(w, core, where)
        remote(slab, slab, w_send, w_recv.at[w, sem], me_loop, sib_dp).wait_recv()

    def kind_z(kind):
        offset = -kind if kind <= 4 else kind - 4
        return lax.rem(zed + offset * sgn + N_Z, N_Z)

    def begin(w):
        to_z(w, zed, 1, 0)
        to_z(w, zed, -1, 4)
        to_x(w, zed, 7)
        if w == 1:
            to_y(chip, 0)
        to_sibling(w, chip)

    def z_arrival(w, kind):
        sem = kind - 1
        where_z = kind_z(kind)
        await_slab(w, where_z * 2 + xlo, sem)
        if kind in (1, 2, 3):
            to_z(w, where_z, 1, sem + 1)
        if kind in (5, 6):
            to_z(w, where_z, -1, sem + 1)
        to_x(w, where_z, 7 + kind)
        if w == 1:
            to_y(where_z * 2 + xlo, kind)
        to_sibling(w, where_z * 2 + xlo)

    def x_arrival(w, kind):
        where = kind_z(kind) * 2 + 1 - xlo
        await_slab(w, where, 7 + kind)
        if w == 1:
            to_y(where, 8 + kind)
        to_sibling(w, where)

    def y_arrival(index):
        side = xlo if index < 8 else 1 - xlo
        where = kind_z(index % 8) * 2 + side
        slab = slab_of(2, core, where)
        remote(slab, slab, y_send, y_recv.at[index], me_loop, sib_dp).wait_recv()
        to_sibling(2, where)

    def kinds_at(step):
        z_kinds = [step] if step <= 4 else []
        z_kinds += [4 + step] if step <= 3 else []
        x_kinds = {1: [0], 5: [4]}.get(step, [step - 1, 3 + step])
        return z_kinds, x_kinds

    def turn(w, step):
        if w == 2 and step == 0:
            y_arrival(0)
            return
        z_kinds, x_kinds = kinds_at(step)
        for kind in z_kinds:
            if w == 2:
                y_arrival(kind)
            else:
                z_arrival(w, kind)
        for kind in x_kinds:
            if w == 2:
                y_arrival(8 + kind)
            else:
                x_arrival(w, kind)

    def sixteen(w):
        return up_buf.at[0] if w == 0 else mix_buf.at[0, :, 0]

    def finish(w):
        whole(sixteen(w), bulk_send.at[w], bulk_recv.at[w]).wait_recv()

    pre_copy = remote(
        pre.at[0, 1 - core], pre.at[1, 0], pre_sem.at[0], pre_sem.at[1], me_loop, sib_dp
    )
    pre_copy.start()

    def text_copy(o):
        return remote(
            text_buf.at[me_loop],
            text_buf.at[me_loop],
            text_sem.at[0],
            text_sem.at[1],
            lax.rem(me_loop + o, N_LOOP),
            me_dp,
        )

    def merge(index):
        mine = pre[0, core, index].astype(F32)[:24]
        theirs = pre[1, 0, index].astype(F32)[:24]
        first = core == 0
        joined = jnp.concatenate(
            [jnp.where(first, mine, theirs), jnp.where(first, theirs, mine)], axis=0
        )
        return joined.astype(BF)

    pre_copy.wait_recv()
    up_buf[core, chip] = merge(0)
    begin(0)
    own_mix = jnp.where(parity == 0, w_down[...].astype(F32), merge(1).astype(F32))
    mix_buf[parity, chip, core] = own_mix.astype(BF)

    @pl.loop(1, N_LOOP)
    def _(o):
        text_copy(o).start()

    width_at = lax.broadcasted_iota(jnp.int32, (16, 128), 0)

    def chunk_lanes(cb):
        return pl.ds(pl.multiple_of(cb * 128, 128), 128)

    def conv_chunk(chunk, carry):
        image, cb = chunk // 6, lax.rem(chunk, 6)
        lanes = chunk_lanes(cb)
        for a in range(7):
            for b in range(7):
                taps[a * 7 + b] = jnp.broadcast_to(kern[a, pl.ds(b, 1), lanes], (8, 128))

        def row(r, state):
            accs, total = state
            x = images[image, r, :, lanes].astype(F32)
            views = []
            for b in range(7):
                if b == 3:
                    view = x
                else:
                    view = pltpu.roll(x, (3 - b) % 16, 0)
                    inside = width_at >= 3 - b if b < 3 else width_at < 19 - b
                    view = jnp.where(inside, view, 0.0)
                shifted[chunk, b, r] = view
                views.append(view.reshape(2, 8, 128))
            fresh = []
            for j in range(7):
                acc = accs[j]
                for b in range(7):
                    acc = acc + views[b] * taps[(6 - j) * 7 + b]
                fresh.append(acc)
            conv_pad[image, r, :, lanes] = fresh[0].reshape(16, 128)
            return (tuple(fresh[1:]) + (jnp.zeros((2, 8, 128), F32),), total + views[3])

        zero = jnp.zeros((2, 8, 128), F32)
        accs, total = lax.fori_loop(0, 16, row, ((zero,) * 7, zero))
        for j in range(3):
            conv_pad[image, 16 + j, :, lanes] = accs[j].reshape(16, 128)
        img_sum[image, :, lanes] = total[0] + total[1]
        return carry

    plan = (
        ((0, 1),),
        ((0, 2), (1, 1)),
        ((0, 3), (1, 2), (2, 0)),
        ((0, 4), (1, 3), (2, 1)),
        ((0, 5), (1, 4), (2, 2)),
        ((1, 5), (2, 3)),
    )
    for group in range(6):
        lax.fori_loop(2 * group, 2 * group + 2, conv_chunk, 0)
        for w, step in plan[group]:
            turn(w, step)
        if group == 0:
            begin(1)

    gain_row = gain[...].reshape(1, C)

    def norm_rows(index, carry):
        image, r = index // 16, lax.rem(index, 16)
        rows = pl.ds(pl.multiple_of(index * 16, 16), 16)
        value = conv_pad[image, r + 3]
        centered = value - jnp.mean(value, axis=-1, keepdims=True)
        inv = lax.rsqrt(jnp.mean(centered * centered, axis=-1, keepdims=True) + EPS)
        hat = centered * inv
        xhat[rows, :] = hat
        rstd[rows, :] = jnp.broadcast_to(inv, (16, 128))
        normed[rows, :] = (hat * gain_row).astype(BF)
        return carry

    lax.fori_loop(0, 32, norm_rows, 0)
    finish(0)

    scale_row = scale[...].reshape(1, C)
    c0 = 0.7978845608028654
    row_at = lax.broadcasted_iota(jnp.int32, (16, C), 0)
    means = []
    for half in range(2):
        hid[...] = jnp.dot(
            normed[...], up_buf[half].reshape(C, C), preferred_element_type=F32
        )
        turn(2, 4 + half)
        bias = b_up[half * C : (half + 1) * C].reshape(1, C)
        image_sums = []
        for image in range(2):

            def gelu_rows(index, total):
                rows = pl.ds(pl.multiple_of(image * 256 + index * 16, 16), 16)
                h = hid[rows, :] + bias
                square = h * h
                t = jnp.tanh(c0 * h * (1.0 + 0.044715 * square))
                plus = 0.5 + 0.5 * t
                active = (h * plus).astype(BF).astype(F32)
                gprime[half, rows, :] = plus + (0.5 * c0) * h * (1.0 - t * t) * (
                    1.0 + (3 * 0.044715) * square
                )
                return total + active[:8] + active[8:]

            total = lax.fori_loop(0, 16, gelu_rows, jnp.zeros((8, C), F32))
            image_sums.append(jnp.sum(total, axis=0, keepdims=True) * (1.0 / 256))
        means.append(
            jnp.where(row_at == 0, image_sums[0], jnp.where(row_at == 1, image_sums[1], 0.0))
        )

    finish(1)
    finish(2)
    mlp = jnp.zeros((16, C), F32)
    for half in range(2):
        high = means[half].astype(BF)
        low = (means[half] - high.astype(F32)).astype(BF)
        rows = mix_buf[0, 8 * half : 8 * half + 8].reshape(C, C)
        mlp = mlp + jnp.dot(high, rows, preferred_element_type=F32)
        mlp = mlp + jnp.dot(low, rows, preferred_element_type=F32)
    img_mean = [jnp.sum(img_sum[image], axis=0, keepdims=True) * (1.0 / 256) for image in range(2)]
    img_mean = jnp.where(row_at == 0, img_mean[0], jnp.where(row_at == 1, img_mean[1], 0.0))
    pooled = (img_mean + scale_row * mlp).astype(BF)
    raw = [
        jnp.dot(
            pooled, mix_buf[1, :, half, :, :EH].reshape(C, EH), preferred_element_type=F32
        )
        for half in range(2)
    ]
    norm = lax.rsqrt(
        jnp.sum(raw[0] * raw[0], axis=-1, keepdims=True)
        + jnp.sum(raw[1] * raw[1], axis=-1, keepdims=True)
        + EPS
    )
    emb = jnp.concatenate([raw[0] * norm, raw[1][:, : E - EH] * norm], axis=1)

    whole(text_buf.at[pl.ds(0, N_LOOP - 1)], text_sem.at[0], text_sem.at[1]).wait_recv()
    for l in range(N_LOOP):
        text_all[2 * l : 2 * l + 2, :] = text_buf[l]
    raw_rows = text_all[...]
    text_norm = jnp.sqrt(jnp.sum(raw_rows * raw_rows, axis=-1, keepdims=True) + EPS)
    text_emb = (raw_rows / text_norm).astype(BF).astype(F32)
    logit_scale = jnp.exp(jnp.full((1, 1), log_temp[0], F32))
    logits = logit_scale * nt(emb, text_emb, HI) + loss_bias[0]
    pair_row_at = lax.broadcasted_iota(jnp.int32, (16, GROUP), 0)
    pair_col_at = lax.broadcasted_iota(jnp.int32, (16, GROUP), 1)
    own = jnp.where(pair_row_at == 0, pair[0, 0], pair[0, 1])
    signs = jnp.where(own == pair_col_at, 1.0, -1.0)
    weight = -signs * jax.nn.sigmoid(-signs * logits) / GROUP
    weight = jnp.where(pair_row_at < 2, weight, 0.0)
    image_cot = logit_scale * jnp.dot(weight, text_emb, precision=HI, preferred_element_type=F32)

    msg_buf[me_loop, :, :E] = emb[:2]
    msg_buf[me_loop, :, E:] = jnp.concatenate(
        [weight[:2], jnp.zeros((2, 128 - GROUP), F32)], axis=1
    )

    def msg_copy(o):
        return remote(
            msg_buf.at[me_loop],
            msg_buf.at[me_loop],
            msg_sem.at[0],
            msg_sem.at[1],
            lax.rem(me_loop + o, N_LOOP),
            me_dp,
        )

    d_raw = norm * (image_cot - emb * jnp.sum(image_cot * emb, axis=-1, keepdims=True))
    d_raw = d_raw.astype(BF)
    d_pooled = nt(d_raw[:, :EH], mix_buf[1, :, 0, :, :EH].reshape(C, EH)) + nt(
        d_raw[:, EH:], mix_buf[1, :, 1, :, : E - EH].reshape(C, E - EH)
    )
    d_pooled = d_pooled.astype(BF).astype(F32)
    d_mlp = (scale_row * (d_pooled * (1.0 / 256))).astype(BF)
    for half in range(2):
        value = nt(d_mlp, mix_buf[0, 8 * half : 8 * half + 8].reshape(C, C))
        dact[half] = value.astype(BF).astype(F32)

    def hidden_cot(half):
        for image in range(2):
            factor = dact[half, image : image + 1, :]

            def rows_cot(index, carry):
                rows = pl.ds(pl.multiple_of(image * 256 + index * 16, 16), 16)
                dhid[half, rows, :] = (gprime[half, rows, :] * factor).astype(BF)
                return carry

            lax.fori_loop(0, 16, rows_cot, 0)

    def up_grad_half(half):
        hidden_cot(half)
        g_buf[half] = tn(normed[...], dhid[half]).astype(BF).reshape(16, 48, C)

    up_grad_half(1 - core)
    r1 = remote(g_buf.at[1 - core], rs1, r1_sem.at[0], r1_sem.at[1], me_loop, sib_dp)
    r1.start()
    up_grad_half(core)
    r1.wait_recv()

    def core_sum(where):
        s1[where] = (g_buf[core, where].astype(F32) + rs1[where].astype(F32)).astype(BF)

    def x_copy(z):
        where = z * 2 + 1 - xlo
        target = me_loop + lax.rem(z, 2) * (loop_b - me_loop)
        return remote(s1.at[where], rs2.at[z], r2_send, r2_recv.at[z], target, xnb_dp)

    @pl.loop(1, N_Z + 1)
    def _(o):
        z = lax.rem(zed + o, N_Z)
        core_sum(z * 2 + 1 - xlo)
        x_copy(z).start()

    @pl.loop(0, N_Z)
    def _(z):
        core_sum(z * 2 + xlo)

    @pl.loop(1, N_LOOP)
    def _(o):
        msg_copy(o).start()

    hid[...] = nt(dhid[0], up_buf[0].reshape(C, C)) + nt(dhid[1], up_buf[1].reshape(C, C))

    dconv = conv_pad

    def norm_cot(index, carry):
        rows = pl.ds(pl.multiple_of(index * 16, 16), 16)
        d_hat = hid[rows, :].astype(BF).astype(F32) * gain_row
        hat = xhat[rows, :]
        first = jnp.mean(d_hat, axis=-1, keepdims=True)
        second = jnp.mean(d_hat * hat, axis=-1, keepdims=True)
        dconv[index // 16, lax.rem(index, 16)] = rstd[rows, :1] * (
            d_hat - first - hat * second
        )
        return carry

    lax.fori_loop(0, 32, norm_cot, 0)

    def z_copy(o):
        z = lax.rem(zed + o, N_Z)
        return remote(
            s2.at[z],
            rs3.at[o - 1],
            r3_sem.at[0],
            r3_sem.at[1],
            me_loop,
            z * 4 + xlo * 2 + core,
        )

    def x_sum(z):
        x_copy(z).wait_recv()
        s2[z] = (s1[z * 2 + xlo].astype(F32) + rs2[z].astype(F32)).astype(BF)

    @pl.loop(1, N_Z)
    def _(o):
        x_sum(lax.rem(zed + o, N_Z))
        z_copy(o).start()

    x_sum(zed)

    kg[...] = jnp.zeros(kg.shape, F32)

    def slab_copy(slab):
        return remote(
            kg.at[slab], kr1.at[me_dp], p1_sem.at[0], p1_sem.at[1], me_loop, slab
        )

    tap_at = lax.broadcasted_iota(jnp.int32, (8, 128), 0)

    def kernel_chunk(cb, offset):
        lanes = chunk_lanes(cb)

        def column(b, carry):
            accs = [jnp.zeros((2, 8, 128), F32) for _ in range(7)]
            for image in range(2):
                window = {}
                for r in range(16):
                    view = shifted[image * 6 + cb, b, r].reshape(2, 8, 128)
                    for a in range(7):
                        h = r - a + 3
                        if 0 <= h < 16:
                            if h not in window:
                                value = dconv[image, h, :, lanes]
                                window[h] = value.reshape(2, 8, 128)
                            accs[a] = accs[a] + view * window[h]
            slab0 = (cb // 2) * 7
            for a in range(7):
                value = jnp.sum(accs[a][0] + accs[a][1], axis=0, keepdims=True)
                columns = slice(offset, offset + 128)
                kg[slab0 + a, :, columns] = kg[slab0 + a, :, columns] + jnp.where(
                    tap_at == b, value, 0.0
                )
            return carry

        lax.fori_loop(0, 7, column, 0)

    for group in range(3):
        kernel_chunk(2 * group, 0)
        kernel_chunk(2 * group + 1, 128)
        for a in range(7):
            slab = group * 7 + a

            @pl.when(me_dp != slab)
            def _():
                slab_copy(slab).start()

    whole(msg_buf.at[pl.ds(0, N_LOOP - 1)], msg_sem.at[0], msg_sem.at[1]).wait_recv()
    for l in range(N_LOOP):
        msg_all[2 * l : 2 * l + 2, :] = msg_buf[l]
    all_emb = msg_all[:, :E]
    all_weight = msg_all[:, E:]
    pick_row = lax.broadcasted_iota(jnp.int32, (8, 128), 0)
    pick_col = lax.broadcasted_iota(jnp.int32, (8, 128), 1)
    pick = jnp.where((pick_col == 2 * me_loop + pick_row) & (pick_row < 2), 1.0, 0.0)
    mine = nt(pick, all_weight, HI)
    text_cot = logit_scale * jnp.dot(mine, all_emb, precision=HI, preferred_element_type=F32)
    text_cot = text_cot[:2]
    own_rows = text[...].astype(F32)
    own_norm = jnp.sqrt(jnp.sum(own_rows * own_rows, axis=-1, keepdims=True) + EPS)
    own_hat = own_rows / own_norm
    text_out[...] = (
        text_cot - own_hat * jnp.sum(own_hat * text_cot, axis=-1, keepdims=True)
    ) / own_norm

    def share_copy(o):
        return remote(
            kr2.at[me_loop],
            kr2.at[me_loop],
            p2_sem.at[0],
            p2_sem.at[1],
            lax.rem(me_loop + o, N_LOOP),
            me_dp,
        )

    @pl.when(me_dp < N_SLAB)
    def _():
        whole(kr1.at[pl.ds(0, N_DP - 1)], p1_sem.at[0], p1_sem.at[1]).wait_recv()
        kr1[me_dp] = kg[me_dp]
        summed = kr1[0]
        for d in range(1, N_DP):
            summed = summed + kr1[d]
        kr2[me_loop] = summed

        @pl.loop(1, N_LOOP)
        def _(o):
            share_copy(o).start()

    total = s2[zed].astype(F32)
    whole(rs3, r3_sem.at[0], r3_sem.at[1]).wait_recv()
    for o in range(1, N_Z):
        total = total + rs3[o - 1].astype(F32)
    for q in range(N_PIECE):
        rb, lh = q // 2, q % 2
        p3[q] = total[rb * 8 : rb * 8 + 8, lh * 384 : lh * 384 + 384]

    def piece_copy(q):
        return remote(p3.at[q], rs4.at[me_loop], r4_sem.at[0], r4_sem.at[1], q, me_dp)

    for q in range(N_PIECE):

        @pl.when(me_loop != q)
        def _():
            piece_copy(q).start()

    def spread_copy(o):
        return remote(
            k1,
            kfin.at[me_dp],
            p3_sem.at[0],
            p3_sem.at[1],
            me_loop,
            lax.rem(me_dp + o, N_DP),
        )

    @pl.when(me_dp < N_SLAB)
    def _():
        whole(kr2.at[pl.ds(0, N_LOOP - 1)], p2_sem.at[0], p2_sem.at[1]).wait_recv()
        summed = kr2[0]
        for l in range(1, N_LOOP):
            summed = summed + kr2[l]
        k1[...] = summed

        @pl.loop(1, N_DP)
        def _(o):
            spread_copy(o).start()

        kfin[me_dp] = summed

    target_core = me_loop // 6
    target_dp = chip * 2 + target_core
    own_piece = lax.rem(me_loop, 6)

    def result_copy(o):
        return remote(
            r4,
            fin.at[core * 6 + own_piece],
            r5_sem.at[0],
            r5_sem.at[1],
            lax.rem(me_loop + o, N_LOOP),
            target_dp,
        )

    @pl.when(me_loop < N_PIECE)
    def _():
        whole(rs4.at[pl.ds(0, N_LOOP - 1)], r4_sem.at[0], r4_sem.at[1]).wait_recv()
        rs4[me_loop] = p3[me_loop]
        summed = rs4[0]
        for l in range(1, N_LOOP):
            summed = summed + rs4[l]
        r4[...] = summed

        @pl.loop(1, N_LOOP)
        def _(o):
            result_copy(o).start()

        @pl.when(target_core != core)
        def _():
            remote(
                r4,
                fin.at[core * 6 + own_piece],
                r5_sem.at[0],
                r5_sem.at[1],
                me_loop,
                sib_dp,
            ).start()

        @pl.when(target_core == core)
        def _():
            fin[core * 6 + own_piece] = r4[...]

    own_result = (target_core == core) & (me_loop < N_PIECE)

    @pl.when(own_result)
    def _():
        whole(fin.at[pl.ds(0, N_PIECE - 1)], r5_sem.at[0], r5_sem.at[1]).wait_recv()

    @pl.when(jnp.logical_not(own_result))
    def _():
        whole(fin, r5_sem.at[0], r5_sem.at[1]).wait_recv()

    for cs in range(2):
        for j in range(6):
            rb, lh = j // 2, j % 2
            columns = slice(cs * C + lh * 384, cs * C + lh * 384 + 384)
            up_out[rb * 8 : rb * 8 + 8, columns] = fin[cs * 6 + j]

    @pl.when(me_dp < N_SLAB)
    def _():
        some = pl.ds(0, N_SLAB - 1)
        whole(kfin.at[some], p3_sem.at[0], p3_sem.at[1]).wait_recv()
        whole(kg.at[some], p1_sem.at[0]).wait_send()
        whole(kr2.at[pl.ds(0, N_LOOP - 1)], p2_sem.at[0]).wait_send()
        whole(kr1.at[pl.ds(0, N_DP - 1)], p3_sem.at[0]).wait_send()

    @pl.when(me_dp >= N_SLAB)
    def _():
        whole(kfin, p3_sem.at[0], p3_sem.at[1]).wait_recv()
        whole(kg, p1_sem.at[0]).wait_send()

    for slab in range(N_SLAB):
        lp, a = slab // 7, slab % 7
        kernel_out[a, :, lp * 256 : lp * 256 + 256] = kfin[slab, :7]

    pre_copy.wait_send()
    for w in range(3):
        whole(sixteen(w), bulk_send.at[w]).wait_send()
    for w in range(2):
        whole(up_buf.at[0, pl.ds(0, 7)], z_send.at[w]).wait_send()
        whole(up_buf.at[0, pl.ds(0, 8)], x_send.at[w]).wait_send()
    whole(sixteen(0), y_send).wait_send()
    whole(text_buf.at[pl.ds(0, N_LOOP - 1)], text_sem.at[0]).wait_send()
    whole(msg_buf.at[pl.ds(0, N_LOOP - 1)], msg_sem.at[0]).wait_send()
    r1.wait_send()
    whole(rs2, r2_send).wait_send()
    whole(rs3, r3_sem.at[0]).wait_send()

    @pl.when(me_loop < N_PIECE)
    def _():
        whole(p3.at[pl.ds(0, N_PIECE - 1)], r4_sem.at[0]).wait_send()

        @pl.when(target_core != core)
        def _():
            whole(rs4, r5_sem.at[0]).wait_send()

        @pl.when(target_core == core)
        def _():
            whole(rs4.at[pl.ds(0, N_LOOP - 1)], r5_sem.at[0]).wait_send()

    @pl.when(me_loop >= N_PIECE)
    def _():
        whole(p3, r4_sem.at[0]).wait_send()


def body(
    images,
    kernel,
    ln_gain,
    w_up,
    b_up,
    w_down,
    layer_scale,
    w_head,
    text_rows,
    pair_ids,
    log_temp,
    loss_bias,
):
    vmem = pl.BlockSpec(memory_space=pltpu.VMEM)
    smem = pl.BlockSpec(memory_space=pltpu.SMEM)
    dma = pltpu.SemaphoreType.DMA
    scratch = [
        pltpu.VMEM((2, 2, 2, 32, C), BF),
        pltpu.VMEM((2, 16, 48, C), BF),
        pltpu.VMEM((2, 16, 2, 48, C), BF),
        pltpu.VMEM((N_LOOP, 2, E), F32),
        pltpu.VMEM((GROUP, E), F32),
        pltpu.VMEM((49, 8, 128), F32),
        pltpu.VMEM((12, 7, 16, 16, 128), F32),
        pltpu.VMEM((2, 19, 16, C), F32),
        pltpu.VMEM((2, 8, C), F32),
        pltpu.VMEM((512, C), BF),
        pltpu.VMEM((512, C), F32),
        pltpu.VMEM((512, 128), F32),
        pltpu.VMEM((512, C), F32),
        pltpu.VMEM((2, 512, C), F32),
        pltpu.VMEM((2, 16, C), F32),
        pltpu.VMEM((2, 512, C), BF),
        pltpu.VMEM((2, 16, 48, C), BF),
        pltpu.VMEM((16, 48, C), BF),
        pltpu.VMEM((16, 48, C), BF),
        pltpu.VMEM((8, 48, C), BF),
        pltpu.VMEM((8, 48, C), BF),
        pltpu.VMEM((7, 48, C), BF),
        pltpu.VMEM((N_PIECE, 8, 384), F32),
        pltpu.VMEM((N_LOOP, 8, 384), F32),
        pltpu.VMEM((8, 384), F32),
        pltpu.VMEM((N_PIECE, 8, 384), F32),
        pltpu.VMEM((N_LOOP, 2, E + 128), F32),
        pltpu.VMEM((GROUP, E + 128), F32),
        pltpu.VMEM((N_SLAB, 8, 256), F32),
        pltpu.VMEM((N_DP, 8, 256), F32),
        pltpu.VMEM((8, 256), F32),
        pltpu.VMEM((N_LOOP, 8, 256), F32),
        pltpu.VMEM((N_SLAB, 8, 256), F32),
        dma,
        dma((2, 15)),
        dma((3,)),
        dma((3,)),
        dma((2,)),
        dma((2,)),
        dma,
        dma((16,)),
        dma((2,)),
        dma((2,)),
        dma((2,)),
        dma((2,)),
        dma,
        dma((N_Z,)),
        dma((2,)),
        dma((2,)),
        dma((2,)),
        dma((2,)),
        dma((2,)),
        dma((2,)),
    ]
    kernel_grad, up_grad, text_grad = pl.pallas_call(
        kernel_body,
        out_shape=(
            jax.ShapeDtypeStruct((7, 7, C), F32),
            jax.ShapeDtypeStruct((24, FFW), F32),
            jax.ShapeDtypeStruct((2, E), F32),
        ),
        in_specs=[vmem] * 9 + [smem] * 3,
        out_specs=(vmem, vmem, vmem),
        scratch_shapes=scratch,
        compiler_params=pltpu.CompilerParams(
            collective_id=0, has_side_effects=True, vmem_limit_bytes=56 * 1024 * 1024
        ),
        name="tower_step",
    )(
        images[0],
        kernel,
        ln_gain,
        w_up,
        b_up,
        w_down,
        layer_scale,
        w_head,
        text_rows[0],
        pair_ids,
        log_temp,
        loss_bias,
    )
    return (kernel_grad, up_grad, text_grad[None])


def solution(mesh):
    placed = (
        P("dp", "loop", None, None, None),
        P(),
        P(),
        P("dp", None),
        P(),
        P("dp", None),
        P(),
        P("dp", None),
        P("dp", "loop", None),
        P("dp", "loop"),
        P(),
        P(),
    )
    return jax.shard_map(
        body,
        mesh=mesh,
        in_specs=placed,
        out_specs=(P(), P("dp", None), P("dp", "loop", None)),
        check_vma=False,
    )
```

time: 123 us -> 113 us (0.919)
  Pallas kernels: 116 us -> 108 us
  local copies, waits for them, and re-layouts: 4.78 us -> 2.94 us
    pallas_call x1, Pallas kernels: 116 us -> 108 us  [body(): pl.pallas_call(kernel_body, out_shape=(jax.ShapeDtypeStruct((7, 7, C), F3...]
    reshape x3 -> x0, local copies, waits for them, and re-layouts: 1.76 us -> none  [the longest x1 0.6 us: body(): b_up.reshape(1, FFW)]
    unnamed x13 -> x7, local copies, waits for them, and re-layouts: 3.02 us -> 2.94 us
where the time goes in v2:
time: 113 us
  Pallas kernels  108 us (96%)
  local copies, waits for them, and re-layouts  2.94 us (3%)
  between operations  1.94 us (2%)
    pallas_call x1, Pallas kernels, body(): pl.pallas_call(kernel_body, out_shape=(jax.ShapeDtypeStruct((7, 7, C), F3...  108 us
    unnamed x7, local copies, waits for them, and re-layouts  2.94 us

profile of v2, /device:TPU:1, one launch (start us, length us, event | category | flops | bytes accessed | tf_op | source)
XLA Modules:
  0.0 113.0 jit_solution(14471362312880117549)
XLA Ops:
  1.9 108.1 %tower_step.1 = (f32[7,7,768]{2,1,0:T(8,128)}, f32[24,1536]{1,0:T(8,128)}, f32[2,1152]{1,0:T(2,128)}) custom-call(bf16[2,16,16,768]{3,2,1,0:T(8,128)(2,1)} %bitcast.3, f32[7,7,768]{2,1,0:T(8,128)} %kern.1, f32[768]{0:T(1024)} %gain.1, bf16[24,1536]{1,0:T(8,128)(2,1)} %w_up.1, f32[1536]{0:T(1024)} %b_up.1, bf16[48,768]{1,0:T(8,128)(2,1)} %w_down.1, ...), custom_call_target="tpu_custom_call" | custom-call | tf_op jit(solution)/shard_map/tower_step/pallas_call | solution.py:855
  110.0 0.0 copy-start
  110.0 1.6 %copy.20 = f32[7,7,768]{2,1,0:T(8,128)} copy(f32[7,7,768]{2,1,0:T(8,128)} %get-tuple-element.12) | data formatting | bytes 301056
  111.7 0.0 copy-done
  111.7 0.0 copy-start.1
  111.7 0.7 copy.21
  112.3 0.0 copy-done.1
  112.4 0.6 copy.22
Async XLA Ops:
  110.0 1.6 %copy-start = (f32[24,1536]{1,0:T(8,128)S(1)}, f32[24,1536]{1,0:T(8,128)}, u32[]{:S(2)}) copy-start(f32[24,1536]{1,0:T(8,128)} %get-tuple-element.13) | copy-start | bytes 442372
  111.7 0.7 copy-start.1

commit v3 on v2

--- a/solution.py
+++ b/solution.py
@@ -22,7 +22,7 @@
 EH = 640
 GROUP = 32
 N_PIECE = 12
-N_SLAB = 21
+N_SLAB = 12
 
 
 def nt(a, b, precision=None):
@@ -80,6 +80,7 @@
     msg_buf,
     msg_all,
     kg,
+    kg_out,
     kr1,
     k1,
     kr2,
@@ -290,9 +291,7 @@
     own_mix = jnp.where(parity == 0, w_down[...].astype(F32), merge(1).astype(F32))
     mix_buf[parity, chip, core] = own_mix.astype(BF)
 
-    @pl.loop(1, N_LOOP)
-    def _(o):
-        text_copy(o).start()
+    begin(1)
 
     width_at = lax.broadcasted_iota(jnp.int32, (16, 128), 0)
 
@@ -336,19 +335,21 @@
         return carry
 
     plan = (
-        ((0, 1),),
-        ((0, 2), (1, 1)),
-        ((0, 3), (1, 2), (2, 0)),
-        ((0, 4), (1, 3), (2, 1)),
-        ((0, 5), (1, 4), (2, 2)),
-        ((1, 5), (2, 3)),
+        ((0, 1), (1, 1)),
+        ((0, 2), (1, 2), (2, 0)),
+        ((0, 3), (1, 3), (2, 1)),
+        ((0, 4), (1, 4), (2, 2)),
+        ((0, 5), (1, 5), (2, 3)),
+        ((2, 4),),
     )
     for group in range(6):
         lax.fori_loop(2 * group, 2 * group + 2, conv_chunk, 0)
         for w, step in plan[group]:
             turn(w, step)
-        if group == 0:
-            begin(1)
+
+    @pl.loop(1, N_LOOP)
+    def _(o):
+        text_copy(o).start()
 
     gain_row = gain[...].reshape(1, C)
 
@@ -375,7 +376,8 @@
         hid[...] = jnp.dot(
             normed[...], up_buf[half].reshape(C, C), preferred_element_type=F32
         )
-        turn(2, 4 + half)
+        if half == 0:
+            turn(2, 5)
         bias = b_up[half * C : (half + 1) * C].reshape(1, C)
         image_sums = []
         for image in range(2):
@@ -549,9 +551,16 @@
 
     kg[...] = jnp.zeros(kg.shape, F32)
 
+    summing = (chip < N_SLAB) & (core == lax.rem(chip, 2))
+
     def slab_copy(slab):
         return remote(
-            kg.at[slab], kr1.at[me_dp], p1_sem.at[0], p1_sem.at[1], me_loop, slab
+            kg_out.at[slab],
+            kr1.at[me_dp],
+            p1_sem.at[0],
+            p1_sem.at[1],
+            me_loop,
+            2 * slab + slab % 2,
         )
 
     tap_at = lax.broadcasted_iota(jnp.int32, (8, 128), 0)
@@ -572,11 +581,11 @@
                                 value = dconv[image, h, :, lanes]
                                 window[h] = value.reshape(2, 8, 128)
                             accs[a] = accs[a] + view * window[h]
-            slab0 = (cb // 2) * 7
+            pair = cb // 2
             for a in range(7):
                 value = jnp.sum(accs[a][0] + accs[a][1], axis=0, keepdims=True)
                 columns = slice(offset, offset + 128)
-                kg[slab0 + a, :, columns] = kg[slab0 + a, :, columns] + jnp.where(
+                kg[pair, a, :, columns] = kg[pair, a, :, columns] + jnp.where(
                     tap_at == b, value, 0.0
                 )
             return carry
@@ -586,12 +595,68 @@
     for group in range(3):
         kernel_chunk(2 * group, 0)
         kernel_chunk(2 * group + 1, 128)
-        for a in range(7):
-            slab = group * 7 + a
-
-            @pl.when(me_dp != slab)
+        for part in range(4):
+            slab = group * 4 + part
+            kg_out[slab] = kg[group, 2 * part : 2 * part + 2].reshape(16, 256).astype(BF)
+
+            @pl.when(jnp.logical_not(summing) | (chip != slab))
             def _():
                 slab_copy(slab).start()
+
+    def share_copy(o):
+        return remote(
+            kr2.at[me_loop],
+            kr2.at[me_loop],
+            p2_sem.at[0],
+            p2_sem.at[1],
+            lax.rem(me_loop + o, N_LOOP),
+            me_dp,
+        )
+
+    def spread_copy(o):
+        return remote(
+            k1, kfin.at[chip], p3_sem.at[0], p3_sem.at[1], me_loop, lax.rem(me_dp + o, N_DP)
+        )
+
+    def sum_dp(first, last):
+        @pl.when(summing & (chip >= first) & (chip < last))
+        def _():
+            whole(kr1.at[pl.ds(0, N_DP - 1)], p1_sem.at[0], p1_sem.at[1]).wait_recv()
+            kr1[me_dp] = kg_out[chip]
+            summed = kr1[0].astype(F32)
+            for d in range(1, N_DP):
+                summed = summed + kr1[d].astype(F32)
+            kr2[me_loop] = summed.astype(BF)
+
+            @pl.loop(1, N_LOOP)
+            def _(o):
+                share_copy(o).start()
+
+    def sum_loop(first, last):
+        @pl.when(summing & (chip >= first) & (chip < last))
+        def _():
+            whole(kr2.at[pl.ds(0, N_LOOP - 1)], p2_sem.at[0], p2_sem.at[1]).wait_recv()
+            summed = kr2[0].astype(F32)
+            for l in range(1, N_LOOP):
+                summed = summed + kr2[l].astype(F32)
+            k1[...] = summed.astype(BF)
+
+            @pl.loop(1, N_DP)
+            def _(o):
+                spread_copy(o).start()
+
+            kfin[chip] = summed.astype(BF)
+
+    sum_dp(0, 8)
+
+    pre_copy.wait_send()
+    for w in range(3):
+        whole(sixteen(w), bulk_send.at[w]).wait_send()
+    for w in range(2):
+        whole(up_buf.at[0, pl.ds(0, 7)], z_send.at[w]).wait_send()
+        whole(up_buf.at[0, pl.ds(0, 8)], x_send.at[w]).wait_send()
+    whole(sixteen(0), y_send).wait_send()
+    whole(text_buf.at[pl.ds(0, N_LOOP - 1)], text_sem.at[0]).wait_send()
 
     whole(msg_buf.at[pl.ds(0, N_LOOP - 1)], msg_sem.at[0], msg_sem.at[1]).wait_recv()
     for l in range(N_LOOP):
@@ -611,29 +676,6 @@
         text_cot - own_hat * jnp.sum(own_hat * text_cot, axis=-1, keepdims=True)
     ) / own_norm
 
-    def share_copy(o):
-        return remote(
-            kr2.at[me_loop],
-            kr2.at[me_loop],
-            p2_sem.at[0],
-            p2_sem.at[1],
-            lax.rem(me_loop + o, N_LOOP),
-            me_dp,
-        )
-
-    @pl.when(me_dp < N_SLAB)
-    def _():
-        whole(kr1.at[pl.ds(0, N_DP - 1)], p1_sem.at[0], p1_sem.at[1]).wait_recv()
-        kr1[me_dp] = kg[me_dp]
-        summed = kr1[0]
-        for d in range(1, N_DP):
-            summed = summed + kr1[d]
-        kr2[me_loop] = summed
-
-        @pl.loop(1, N_LOOP)
-        def _(o):
-            share_copy(o).start()
-
     total = s2[zed].astype(F32)
     whole(rs3, r3_sem.at[0], r3_sem.at[1]).wait_recv()
     for o in range(1, N_Z):
@@ -651,29 +693,8 @@
         def _():
             piece_copy(q).start()
 
-    def spread_copy(o):
-        return remote(
-            k1,
-            kfin.at[me_dp],
-            p3_sem.at[0],
-            p3_sem.at[1],
-            me_loop,
-            lax.rem(me_dp + o, N_DP),
-        )
-
-    @pl.when(me_dp < N_SLAB)
-    def _():
-        whole(kr2.at[pl.ds(0, N_LOOP - 1)], p2_sem.at[0], p2_sem.at[1]).wait_recv()
-        summed = kr2[0]
-        for l in range(1, N_LOOP):
-            summed = summed + kr2[l]
-        k1[...] = summed
-
-        @pl.loop(1, N_DP)
-        def _(o):
-            spread_copy(o).start()
-
-        kfin[me_dp] = summed
+    sum_dp(8, N_SLAB)
+    sum_loop(0, 8)
 
     target_core = me_loop // 6
     target_dp = chip * 2 + target_core
@@ -717,6 +738,8 @@
         def _():
             fin[core * 6 + own_piece] = r4[...]
 
+    sum_loop(8, N_SLAB)
+
     own_result = (target_core == core) & (me_loop < N_PIECE)
 
     @pl.when(own_result)
@@ -733,31 +756,26 @@
             columns = slice(cs * C + lh * 384, cs * C + lh * 384 + 384)
             up_out[rb * 8 : rb * 8 + 8, columns] = fin[cs * 6 + j]
 
-    @pl.when(me_dp < N_SLAB)
+    @pl.when(summing)
     def _():
         some = pl.ds(0, N_SLAB - 1)
         whole(kfin.at[some], p3_sem.at[0], p3_sem.at[1]).wait_recv()
-        whole(kg.at[some], p1_sem.at[0]).wait_send()
+        whole(kg_out.at[some], p1_sem.at[0]).wait_send()
         whole(kr2.at[pl.ds(0, N_LOOP - 1)], p2_sem.at[0]).wait_send()
         whole(kr1.at[pl.ds(0, N_DP - 1)], p3_sem.at[0]).wait_send()
 
-    @pl.when(me_dp >= N_SLAB)
+    @pl.when(jnp.logical_not(summing))
     def _():
         whole(kfin, p3_sem.at[0], p3_sem.at[1]).wait_recv()
-        whole(kg, p1_sem.at[0]).wait_send()
+        whole(kg_out, p1_sem.at[0]).wait_send()
 
     for slab in range(N_SLAB):
-        lp, a = slab // 7, slab % 7
-        kernel_out[a, :, lp * 256 : lp * 256 + 256] = kfin[slab, :7]
-
-    pre_copy.wait_send()
-    for w in range(3):
-        whole(sixteen(w), bulk_send.at[w]).wait_send()
-    for w in range(2):
-        whole(up_buf.at[0, pl.ds(0, 7)], z_send.at[w]).wait_send()
-        whole(up_buf.at[0, pl.ds(0, 8)], x_send.at[w]).wait_send()
-    whole(sixteen(0), y_send).wait_send()
-    whole(text_buf.at[pl.ds(0, N_LOOP - 1)], text_sem.at[0]).wait_send()
+        lp, part = slab // 4, slab % 4
+        value = kfin[slab].astype(F32)
+        kernel_out[2 * part, :, lp * 256 : lp * 256 + 256] = value[:7]
+        if part < 3:
+            kernel_out[2 * part + 1, :, lp * 256 : lp * 256 + 256] = value[8:15]
+
     whole(msg_buf.at[pl.ds(0, N_LOOP - 1)], msg_sem.at[0]).wait_send()
     r1.wait_send()
     whole(rs2, r2_send).wait_send()
@@ -826,11 +844,12 @@
         pltpu.VMEM((N_PIECE, 8, 384), F32),
         pltpu.VMEM((N_LOOP, 2, E + 128), F32),
         pltpu.VMEM((GROUP, E + 128), F32),
-        pltpu.VMEM((N_SLAB, 8, 256), F32),
-        pltpu.VMEM((N_DP, 8, 256), F32),
-        pltpu.VMEM((8, 256), F32),
-        pltpu.VMEM((N_LOOP, 8, 256), F32),
-        pltpu.VMEM((N_SLAB, 8, 256), F32),
+        pltpu.VMEM((3, 8, 8, 256), F32),
+        pltpu.VMEM((N_SLAB, 16, 256), BF),
+        pltpu.VMEM((N_DP, 16, 256), BF),
+        pltpu.VMEM((16, 256), BF),
+        pltpu.VMEM((N_LOOP, 16, 256), BF),
+        pltpu.VMEM((N_SLAB, 16, 256), BF),
         dma,
         dma((2, 15)),
         dma((3,)),

time: 113 us -> 111 us (0.982)
  Pallas kernels: 108 us -> 105 us
    pallas_call x1, Pallas kernels: 108 us -> 105 us  [body(): pl.pallas_call(kernel_body, out_shape=(jax.ShapeDtypeStruct((7, 7, C), F3...]
where the time goes in v3:
time: 111 us; the launch traced here: 110 us
  Pallas kernels  105 us (95%)
  local copies, waits for them, and re-layouts  2.94 us (3%)
  between operations  1.94 us (2%)
    pallas_call x1, Pallas kernels, body(): pl.pallas_call(kernel_body, out_shape=(jax.ShapeDtypeStruct((7, 7, C), F3...  105 us
    unnamed x7, local copies, waits for them, and re-layouts  2.94 us

profile of v3, /device:TPU:1, one launch (start us, length us, event | category | flops | bytes accessed | tf_op | source)
XLA Modules:
  0.0 110.3 jit_solution(3923841648973388538)
XLA Ops:
  1.9 105.4 %tower_step.1 = (f32[7,7,768]{2,1,0:T(8,128)}, f32[24,1536]{1,0:T(8,128)}, f32[2,1152]{1,0:T(2,128)}) custom-call(bf16[2,16,16,768]{3,2,1,0:T(8,128)(2,1)} %bitcast.3, f32[7,7,768]{2,1,0:T(8,128)} %kern.1, f32[768]{0:T(1024)} %gain.1, bf16[24,1536]{1,0:T(8,128)(2,1)} %w_up.1, f32[1536]{0:T(1024)} %b_up.1, bf16[48,768]{1,0:T(8,128)(2,1)} %w_down.1, ...), custom_call_target="tpu_custom_call" | custom-call | tf_op jit(solution)/shard_map/tower_step/pallas_call | solution.py:874
  107.4 0.0 copy-start
  107.4 1.6 %copy.20 = f32[7,7,768]{2,1,0:T(8,128)} copy(f32[7,7,768]{2,1,0:T(8,128)} %get-tuple-element.12) | data formatting | bytes 301056
  109.0 0.0 copy-done
  109.0 0.0 copy-start.1
  109.0 0.7 copy.21
  109.7 0.0 copy-done.1
  109.7 0.6 copy.22
Async XLA Ops:
  107.4 1.6 %copy-start = (f32[24,1536]{1,0:T(8,128)S(1)}, f32[24,1536]{1,0:T(8,128)}, u32[]{:S(2)}) copy-start(f32[24,1536]{1,0:T(8,128)} %get-tuple-element.13) | copy-start | bytes 442372
  109.0 0.7 copy-start.1

commit v4 on v3

--- a/solution.py
+++ b/solution.py
@@ -486,6 +486,11 @@
     r1 = remote(g_buf.at[1 - core], rs1, r1_sem.at[0], r1_sem.at[1], me_loop, sib_dp)
     r1.start()
     up_grad_half(core)
+
+    @pl.loop(1, N_LOOP)
+    def _(o):
+        msg_copy(o).start()
+
     r1.wait_recv()
 
     def core_sum(where):
@@ -505,10 +510,6 @@
     @pl.loop(0, N_Z)
     def _(z):
         core_sum(z * 2 + xlo)
-
-    @pl.loop(1, N_LOOP)
-    def _(o):
-        msg_copy(o).start()
 
     hid[...] = nt(dhid[0], up_buf[0].reshape(C, C)) + nt(dhid[1], up_buf[1].reshape(C, C))
 
@@ -542,12 +543,10 @@
         x_copy(z).wait_recv()
         s2[z] = (s1[z * 2 + xlo].astype(F32) + rs2[z].astype(F32)).astype(BF)
 
-    @pl.loop(1, N_Z)
+    @pl.loop(1, 5)
     def _(o):
         x_sum(lax.rem(zed + o, N_Z))
         z_copy(o).start()
-
-    x_sum(zed)
 
     kg[...] = jnp.zeros(kg.shape, F32)
 
@@ -595,6 +594,15 @@
     for group in range(3):
         kernel_chunk(2 * group, 0)
         kernel_chunk(2 * group + 1, 128)
+        if group == 0:
+
+            @pl.loop(5, N_Z)
+            def _(o):
+                x_sum(lax.rem(zed + o, N_Z))
+                z_copy(o).start()
+
+            x_sum(zed)
+
         for part in range(4):
             slab = group * 4 + part
             kg_out[slab] = kg[group, 2 * part : 2 * part + 2].reshape(16, 256).astype(BF)

time: 111 us -> 110 us (level)
  no operation moved by 1% of the time
where the time goes in v4:
time: 110 us
  Pallas kernels  105 us (95%)
  local copies, waits for them, and re-layouts  2.94 us (3%)
  between operations  1.94 us (2%)
    pallas_call x1, Pallas kernels, body(): pl.pallas_call(kernel_body, out_shape=(jax.ShapeDtypeStruct((7, 7, C), F3...  105 us
    unnamed x7, local copies, waits for them, and re-layouts  2.94 us

profile of v4, /device:TPU:1, one launch (start us, length us, event | category | flops | bytes accessed | tf_op | source)
XLA Modules:
  0.0 110.1 jit_solution(7698972196563446720)
XLA Ops:
  1.9 105.2 %tower_step.1 = (f32[7,7,768]{2,1,0:T(8,128)}, f32[24,1536]{1,0:T(8,128)}, f32[2,1152]{1,0:T(2,128)}) custom-call(bf16[2,16,16,768]{3,2,1,0:T(8,128)(2,1)} %bitcast.3, f32[7,7,768]{2,1,0:T(8,128)} %kern.1, f32[768]{0:T(1024)} %gain.1, bf16[24,1536]{1,0:T(8,128)(2,1)} %w_up.1, f32[1536]{0:T(1024)} %b_up.1, bf16[48,768]{1,0:T(8,128)(2,1)} %w_down.1, ...), custom_call_target="tpu_custom_call" | custom-call | tf_op jit(solution)/shard_map/tower_step/pallas_call | solution.py:882
  107.2 0.0 copy-start
  107.2 1.6 %copy.20 = f32[7,7,768]{2,1,0:T(8,128)} copy(f32[7,7,768]{2,1,0:T(8,128)} %get-tuple-element.12) | data formatting | bytes 301056
  108.8 0.0 copy-done
  108.8 0.0 copy-start.1
  108.8 0.7 copy.21
  109.5 0.0 copy-done.1
  109.5 0.6 copy.22
Async XLA Ops:
  107.2 1.6 %copy-start = (f32[24,1536]{1,0:T(8,128)S(1)}, f32[24,1536]{1,0:T(8,128)}, u32[]{:S(2)}) copy-start(f32[24,1536]{1,0:T(8,128)} %get-tuple-element.13) | copy-start | bytes 442372
  108.8 0.7 copy-start.1

commit v5 on v3

--- a/solution.py
+++ b/solution.py
@@ -400,6 +400,15 @@
             jnp.where(row_at == 0, image_sums[0], jnp.where(row_at == 1, image_sums[1], 0.0))
         )
 
+    whole(text_buf.at[pl.ds(0, N_LOOP - 1)], text_sem.at[0], text_sem.at[1]).wait_recv()
+    for l in range(N_LOOP):
+        text_all[2 * l : 2 * l + 2, :] = text_buf[l]
+    raw_rows = text_all[...]
+    text_norm = jnp.sqrt(jnp.sum(raw_rows * raw_rows, axis=-1, keepdims=True) + EPS)
+    text_emb = (raw_rows / text_norm).astype(BF).astype(F32)
+    logit_scale = jnp.exp(jnp.full((1, 1), log_temp[0], F32))
+    img_mean = [jnp.sum(img_sum[image], axis=0, keepdims=True) * (1.0 / 256) for image in range(2)]
+    img_mean = jnp.where(row_at == 0, img_mean[0], jnp.where(row_at == 1, img_mean[1], 0.0))
     finish(1)
     finish(2)
     mlp = jnp.zeros((16, C), F32)
@@ -409,8 +418,6 @@
         rows = mix_buf[0, 8 * half : 8 * half + 8].reshape(C, C)
         mlp = mlp + jnp.dot(high, rows, preferred_element_type=F32)
         mlp = mlp + jnp.dot(low, rows, preferred_element_type=F32)
-    img_mean = [jnp.sum(img_sum[image], axis=0, keepdims=True) * (1.0 / 256) for image in range(2)]
-    img_mean = jnp.where(row_at == 0, img_mean[0], jnp.where(row_at == 1, img_mean[1], 0.0))
     pooled = (img_mean + scale_row * mlp).astype(BF)
     raw = [
         jnp.dot(
@@ -425,13 +432,6 @@
     )
     emb = jnp.concatenate([raw[0] * norm, raw[1][:, : E - EH] * norm], axis=1)
 
-    whole(text_buf.at[pl.ds(0, N_LOOP - 1)], text_sem.at[0], text_sem.at[1]).wait_recv()
-    for l in range(N_LOOP):
-        text_all[2 * l : 2 * l + 2, :] = text_buf[l]
-    raw_rows = text_all[...]
-    text_norm = jnp.sqrt(jnp.sum(raw_rows * raw_rows, axis=-1, keepdims=True) + EPS)
-    text_emb = (raw_rows / text_norm).astype(BF).astype(F32)
-    logit_scale = jnp.exp(jnp.full((1, 1), log_temp[0], F32))
     logits = logit_scale * nt(emb, text_emb, HI) + loss_bias[0]
     pair_row_at = lax.broadcasted_iota(jnp.int32, (16, GROUP), 0)
     pair_col_at = lax.broadcasted_iota(jnp.int32, (16, GROUP), 1)

time: 111 us -> 111 us (level)
  no operation moved by 1% of the time
where the time goes in v5:
time: 111 us; the launch traced here: 110 us
  Pallas kernels  105 us (95%)
  local copies, waits for them, and re-layouts  2.94 us (3%)
  between operations  1.94 us (2%)
    pallas_call x1, Pallas kernels, body(): pl.pallas_call(kernel_body, out_shape=(jax.ShapeDtypeStruct((7, 7, C), F3...  105 us
    unnamed x7, local copies, waits for them, and re-layouts  2.94 us

profile of v5, /device:TPU:1, one launch (start us, length us, event | category | flops | bytes accessed | tf_op | source)
XLA Modules:
  0.0 110.3 jit_solution(15643187272876794310)
XLA Ops:
  1.9 105.4 %tower_step.1 = (f32[7,7,768]{2,1,0:T(8,128)}, f32[24,1536]{1,0:T(8,128)}, f32[2,1152]{1,0:T(2,128)}) custom-call(bf16[2,16,16,768]{3,2,1,0:T(8,128)(2,1)} %bitcast.3, f32[7,7,768]{2,1,0:T(8,128)} %kern.1, f32[768]{0:T(1024)} %gain.1, bf16[24,1536]{1,0:T(8,128)(2,1)} %w_up.1, f32[1536]{0:T(1024)} %b_up.1, bf16[48,768]{1,0:T(8,128)(2,1)} %w_down.1, ...), custom_call_target="tpu_custom_call" | custom-call | tf_op jit(solution)/shard_map/tower_step/pallas_call | solution.py:874
  107.4 0.0 copy-start
  107.4 1.6 %copy.20 = f32[7,7,768]{2,1,0:T(8,128)} copy(f32[7,7,768]{2,1,0:T(8,128)} %get-tuple-element.12) | data formatting | bytes 301056
  109.0 0.0 copy-done
  109.0 0.0 copy-start.1
  109.0 0.7 copy.21
  109.7 0.0 copy-done.1
  109.7 0.6 copy.22
Async XLA Ops:
  107.4 1.6 %copy-start = (f32[24,1536]{1,0:T(8,128)S(1)}, f32[24,1536]{1,0:T(8,128)}, u32[]{:S(2)}) copy-start(f32[24,1536]{1,0:T(8,128)} %get-tuple-element.13) | copy-start | bytes 442372
  109.0 0.7 copy-start.1
